TPU v7x, 256 devices: a whole 4x4x8 slice. The times are simulated.
256 devices in a mesh: lat: 16 (over x, y), lon: 16 (over z, core).
Axes of the slice: x: 4, y: 4, z: 8, core: 2. Of those that a mesh axis runs over, the one named last changes fastest.
Arguments:
- start_block: float32 [512, 8, 2, 1025], P(('lat', 'lon')), may hold values from -6 to 6
- legendre: bfloat16 [512, 1024, 1025], P('lat', 'lon'), may hold values from -0.1875 to 0.1875
- variance: float32 [1024, 2048], P('lon', 'lat'), may hold values from 0.25 to 4
- gauss_weight: float32 [1024], P('lon'), may hold values from 0.1 to 1.9
- pair_of_slot: int32 [512], replicated, may hold values from 0 to 511, each once
Outputs:
- modes: float32 [512, 8, 2, 1025], P(('lat', 'lon'))
- factor: float32 [8, 8], replicated
Inputs may be any that keep to these rules, and one draw needn't show every extreme that they name: `pair_of_slot`: each pair number appears in exactly one slot.
All inputs are finite; a program needn't handle non-finite values.
Results may differ from a plain program's by a relative error of at most 0.025.
Values may be sent and summed in bfloat16 or wider, within the bound.
No kernel may reach another device: no remote copies, remote signals or barrier semaphores. Data moves between devices by JAX's collectives and lax.ppermute only.
A program may use at most 64 MiB of HBM per device.

v0:
```python
import math

import jax
import jax.numpy as jnp
from jax import lax
from jax.sharding import PartitionSpec as P

T_SIZE = 1023
NLON = 2048
K = 8
STEPS = 3
NPAIR = 512
R = 1025


def pair_layout(pair_ids, width):
    places = jnp.arange(width, dtype=jnp.int32)
    cut = T_SIZE + 1 - pair_ids
    first = places[None, :] < cut[:, None]
    degree = jnp.where(first, pair_ids[:, None] + places[None, :], places[None, :] - 1)
    return (first, degree)


def spectral_factor(degree):
    level = degree.astype(jnp.float32)
    return lax.rsqrt(1.0 + level * (level + 1.0) * (4.0 / (T_SIZE * T_SIZE)))


def wave_angles(pair_ids, lon_ids):
    waves = jnp.stack([pair_ids, T_SIZE - pair_ids], axis=1)
    phase = waves[:, :, None] * lon_ids[None, None, :] % NLON
    return (waves, phase.astype(jnp.float32) * (2.0 * math.pi / NLON))


def inverse_table(pair_ids, lon_ids):
    waves, angle = wave_angles(pair_ids, lon_ids)
    weight = jnp.where(waves == 0, 1.0, 2.0).astype(jnp.float32)[:, :, None, None]
    return (weight * jnp.stack([jnp.cos(angle), -jnp.sin(angle)], axis=2)).astype(jnp.bfloat16)


def forward_table(pair_ids, lon_ids):
    waves, angle = wave_angles(pair_ids, lon_ids)
    return (jnp.stack([jnp.cos(angle), -jnp.sin(angle)], axis=2) * (1.0 / NLON)).astype(
        jnp.bfloat16
    )


def legendre_inverse(spec, legendre, first):
    mask = first[:, None, None, :]
    masked = jnp.stack([jnp.where(mask, spec, 0), jnp.where(mask, 0, spec)], axis=1)
    slots, halves, fields, parts, width = masked.shape
    waves = jnp.einsum(
        "sqr,sjr->sqj",
        masked.reshape(slots, 4 * fields, width),
        legendre,
        preferred_element_type=jnp.float32,
    )
    return waves.reshape(slots, 2, fields, 2, legendre.shape[1]).astype(jnp.bfloat16)


def degree_terms(spectral_grid, legendre, first):
    slots, halves, fields, parts, rows = spectral_grid.shape
    flat = spectral_grid.reshape(slots, 4 * fields, rows)
    projected = jnp.einsum("sqj,sjr->sqr", flat, legendre, preferred_element_type=jnp.float32)
    projected = projected.reshape(slots, 2, fields, 2, legendre.shape[2])
    return jnp.where(first[:, None, None, :], projected[:, 0], projected[:, 1])


def gram_of(shaped):
    return jnp.einsum("skcr,sqcr->kq", shaped, shaped, precision=lax.Precision.HIGHEST)


def orthonormal(shaped, gram):
    gram = gram / (2.0 * NPAIR * R)
    lower = jnp.linalg.cholesky(gram)
    inverse = jax.scipy.linalg.solve_triangular(lower, jnp.eye(K, dtype=jnp.float32), lower=True)
    current = jnp.einsum("kq,sqcr->skcr", inverse, shaped, precision=lax.Precision.HIGHEST)
    return (lower, current)


def body(start_block, legendre, variance, gauss_weight, pair_of_slot):
    lat_pos = lax.axis_index("lat")
    lon_pos = lax.axis_index("lon")
    per_lat, rows_j, width_r = legendre.shape
    per_dev = start_block.shape[0]
    fields = start_block.shape[1]
    lon_dev = variance.shape[1]
    own_pid = lax.dynamic_slice_in_dim(pair_of_slot, lat_pos * per_lat, per_lat)
    first, degree = pair_layout(own_pid, width_r)
    factor_rows = spectral_factor(degree)
    lon_index = lat_pos * lon_dev + jnp.arange(lon_dev, dtype=jnp.int32)
    weight_col = gauss_weight[None, None, None, None, :]

    def spread(block):
        return lax.all_gather(block.astype(jnp.bfloat16), "lon", axis=0, tiled=True)

    spec = spread(start_block)
    current = start_block
    lower = jnp.zeros((fields, fields), jnp.float32)
    for step in range(STEPS):
        waves = legendre_inverse(spec, legendre, first)
        add_table = inverse_table(pair_of_slot, lon_index)
        grid = jnp.einsum(
            "shkcj,shcl->kjl",
            lax.all_gather(waves, "lat", axis=0, tiled=True),
            add_table,
            preferred_element_type=jnp.float32,
        )
        scaled_grid = (grid * variance[None]).astype(jnp.bfloat16)
        piece = lax.all_gather(scaled_grid, "lat", axis=2, tiled=True)
        lon_ids = jnp.arange(piece.shape[2], dtype=jnp.int32)
        table = forward_table(own_pid, lon_ids)
        summed = jnp.einsum("kjl,shcl->shkcj", piece, table, preferred_element_type=jnp.float32)
        spectral_grid = (summed * weight_col).astype(jnp.bfloat16)
        projected = lax.psum_scatter(
            degree_terms(spectral_grid, legendre, first).astype(jnp.bfloat16),
            "lon",
            scatter_dimension=0,
            tiled=True,
        ).astype(jnp.float32)
        own_factor = lax.dynamic_slice_in_dim(factor_rows, lon_pos * per_dev, per_dev, 0)
        shaped = projected * own_factor[:, None, None, :]
        gram = lax.psum(gram_of(shaped), ("lat", "lon"))
        lower, current = orthonormal(shaped, gram)
        if step + 1 < STEPS:
            spec = spread(current)
    return (current, lower)


def solution(mesh):
    placed = (
        P(("lat", "lon"), None, None, None),
        P("lat", "lon", None),
        P("lon", "lat"),
        P("lon"),
        P(),
    )
    return jax.shard_map(
        body,
        mesh=mesh,
        in_specs=placed,
        out_specs=(P(("lat", "lon"), None, None, None), P()),
        check_vma=False,
    )
```

profile of v0, /device:TPU:1, one launch (start us, length us, event | category | flops | bytes accessed | tf_op | source)
XLA Modules:
  0.0 935.6 jit_solution(15147922129326904664)
XLA Ops:
  7.2 1.6 copy.228
  8.8 0.8 subtract_bitcast_fusion
  9.7 43.8 %all-gather.10.cloned.1.call-done = bf16[32,8,2,1025]{3,1,2,0:T(8,128)(2,1)} async-done(((bf16[2,8,2,1025]{3,1,2,0:T(8,128)(2,1)}), bf16[32,8,2,1025]{3,1,2,0:T(8,128)(2,1)}) %all-gather.10.cloned.1.call-update) | async-done | bytes 1049616 | tf_op jit(solution)/shard_map/all_gather | solution.py:95
  53.5 1.7 select_bitcast_fusion.5
  55.5 2.0 copy-done
  57.5 1.5 fusion.41
  59.0 0.7 copy.114
  59.9 2.1 fusion.108
  62.3 52.5 %all-gather.12.cloned.1.call-done = bf16[512,2,8,2,64]{4,2,3,1,0:T(8,128)(2,1)} async-done(((bf16[32,2,8,2,64]{4,2,3,1,0:T(8,128)(2,1)}), bf16[512,2,8,2,64]{4,2,3,1,0:T(8,128)(2,1)}) %all-gather.12.cloned.1.call-update) | async-done | bytes 2097168 | tf_op jit(solution)/shard_map/all_gather | solution.py:105
  114.7 5.1 fusion.80
  120.1 2.1 fusion.109
  122.3 49.3 %all-gather.14.cloned.1.call-done = bf16[8,64,2048]{2,1,0:T(8,128)(2,1)} async-done(((bf16[8,64,128]{2,1,0:T(8,128)(2,1)}), bf16[8,64,2048]{2,1,0:T(8,128)(2,1)}) %all-gather.14.cloned.1.call-update) | async-done | bytes 2097168 | tf_op jit(solution)/shard_map/all_gather | solution.py:110
  171.6 2.8 fusion.53
  174.4 3.2 fusion.106
  177.6 0.7 copy.172
  178.5 1.7 copy.120
  180.4 55.1 %reduce-scatter.4.cloned.1.call-done = bf16[2,8,2,1025]{3,1,2,0:T(8,128)(2,1)} async-done(((bf16[32,8,2,1025]{3,1,2,0:T(8,128)(2,1)}), bf16[2,8,2,1025]{3,1,2,0:T(8,128)(2,1)}) %reduce-scatter.4.cloned.1.call-update) | async-done | bytes 65616 | tf_op jit(solution)/shard_map/reduce_scatter | solution.py:115
  235.5 1.4 convolution_bitcast_fusion.6
  236.8 79.8 %psum.21 = f32[8,8]{0,1:T(8,128)S(1)} all-reduce(f32[8,8]{0,1:T(8,128)S(1)} %convolution_bitcast_fusion.6), channel_id=1, replica_groups=mesh['lat'=16,'lon'=16] {'lat','lon'}, use_global_device_ids=true, to_apply=%region_1.2 | all-reduce | flops 64 | bytes 512 | tf_op jit(solution)/shard_map/psum | solution.py:123
  316.7 0.7 cholesky.59
  317.5 0.6 compare_reduce_fusion.2
  318.1 0.6 fusion.119
  318.8 0.6 custom-call.7
  319.6 1.8 fusion.18
  321.5 35.0 %all-gather.16.cloned.1.call-done = bf16[32,8,2,1025]{3,1,2,0:T(8,128)(2,1)} async-done(((bf16[2,8,2,1025]{3,1,2,0:T(8,128)(2,1)}), bf16[32,8,2,1025]{3,1,2,0:T(8,128)(2,1)}) %all-gather.16.cloned.1.call-update) | async-done | bytes 1049616 | tf_op jit(solution)/shard_map/all_gather | solution.py:95
  356.5 1.7 select_bitcast_fusion.3
  358.5 4.0 fusion.35
  362.6 0.7 copy.129
  363.4 54.9 %all-gather.18.cloned.1.call-done = bf16[512,2,8,2,64]{4,2,3,1,0:T(8,128)(2,1)} async-done(((bf16[32,2,8,2,64]{4,2,3,1,0:T(8,128)(2,1)}), bf16[512,2,8,2,64]{4,2,3,1,0:T(8,128)(2,1)}) %all-gather.18.cloned.1.call-update) | async-done | bytes 2097168 | tf_op jit(solution)/shard_map/all_gather | solution.py:105
  418.3 5.1 fusion.83
  423.7 51.4 %all-gather.20.cloned.1.call-done = bf16[8,64,2048]{2,1,0:T(8,128)(2,1)} async-done(((bf16[8,64,128]{2,1,0:T(8,128)(2,1)}), bf16[8,64,2048]{2,1,0:T(8,128)(2,1)}) %all-gather.20.cloned.1.call-update) | async-done | bytes 2097168 | tf_op jit(solution)/shard_map/all_gather | solution.py:110
  475.1 2.8 fusion.56
  477.9 3.2 fusion.104
  481.1 0.7 copy.133
  482.0 1.7 copy.134
  483.7 55.3 %reduce-scatter.6.cloned.1.call-done = bf16[2,8,2,1025]{3,1,2,0:T(8,128)(2,1)} async-done(((bf16[32,8,2,1025]{3,1,2,0:T(8,128)(2,1)}), bf16[2,8,2,1025]{3,1,2,0:T(8,128)(2,1)}) %reduce-scatter.6.cloned.1.call-update) | async-done | bytes 65616 | tf_op jit(solution)/shard_map/reduce_scatter | solution.py:115
  539.0 1.4 convolution_bitcast_fusion.4
  540.4 79.6 %psum.22 = f32[8,8]{0,1:T(8,128)S(1)} all-reduce(f32[8,8]{0,1:T(8,128)S(1)} %convolution_bitcast_fusion.4), channel_id=1, replica_groups=mesh['lat'=16,'lon'=16] {'lat','lon'}, use_global_device_ids=true, to_apply=%region_5.8 | all-reduce | flops 64 | bytes 512 | tf_op jit(solution)/shard_map/psum | solution.py:123
  620.1 0.7 cholesky.70
  620.8 0.6 compare_reduce_fusion.1
  621.5 0.6 fusion.120
  622.1 0.6 custom-call.8
  622.9 1.8 fusion.19
  624.8 35.0 %all-gather.22.cloned.1.call-done = bf16[32,8,2,1025]{3,1,2,0:T(8,128)(2,1)} async-done(((bf16[2,8,2,1025]{3,1,2,0:T(8,128)(2,1)}), bf16[32,8,2,1025]{3,1,2,0:T(8,128)(2,1)}) %all-gather.22.cloned.1.call-update) | async-done | bytes 1049616 | tf_op jit(solution)/shard_map/all_gather | solution.py:95
  659.8 1.7 select_bitcast_fusion.1
  661.8 4.0 fusion.38
  665.9 0.7 copy.143
  666.7 54.9 %all-gather.24.cloned.1.call-done = bf16[512,2,8,2,64]{4,2,3,1,0:T(8,128)(2,1)} async-done(((bf16[32,2,8,2,64]{4,2,3,1,0:T(8,128)(2,1)}), bf16[512,2,8,2,64]{4,2,3,1,0:T(8,128)(2,1)}) %all-gather.24.cloned.1.call-update) | async-done | bytes 2097168 | tf_op jit(solution)/shard_map/all_gather | solution.py:105
  721.6 5.1 fusion.86
  726.7 0.3 reduce-scatter.8.cloned.1.call-start
  727.0 51.4 %all-gather.26.cloned.1.call-done = bf16[8,64,2048]{2,1,0:T(8,128)(2,1)} async-done(((bf16[8,64,128]{2,1,0:T(8,128)(2,1)}), bf16[8,64,2048]{2,1,0:T(8,128)(2,1)}) %all-gather.26.cloned.1.call-update) | async-done | bytes 2097168 | tf_op jit(solution)/shard_map/all_gather | solution.py:110
  778.4 2.8 fusion.59
  781.3 3.2 fusion.102
  784.4 0.7 copy.147
  785.3 1.7 copy.148
  787.0 55.3 %reduce-scatter.8.cloned.1.call-done = bf16[2,8,2,1025]{3,1,2,0:T(8,128)(2,1)} async-done(((bf16[32,8,2,1025]{3,1,2,0:T(8,128)(2,1)}), bf16[2,8,2,1025]{3,1,2,0:T(8,128)(2,1)}) %reduce-scatter.8.cloned.1.call-update) | async-done | bytes 65616 | tf_op jit(solution)/shard_map/reduce_scatter | solution.py:115
  842.3 1.4 convolution_bitcast_fusion.2
  843.7 79.6 %psum.23 = f32[8,8]{0,1:T(8,128)S(1)} all-reduce(f32[8,8]{0,1:T(8,128)S(1)} %convolution_bitcast_fusion.2), channel_id=1, replica_groups=mesh['lat'=16,'lon'=16] {'lat','lon'}, use_global_device_ids=true, to_apply=%region_7.10 | all-reduce | flops 64 | bytes 512 | tf_op jit(solution)/shard_map/psum | solution.py:123
  923.4 0.7 cholesky.81
  924.1 0.6 compare_reduce_fusion
  924.8 1.2 select_bitcast_fusion.6
  926.0 0.6 custom-call.9
  926.8 1.2 convolution_bitcast_fusion
  928.0 0.7 copy.154
  (65 shorter events, 3.8 us)
Async XLA Ops:
  7.2 46.3 %all-gather.10.cloned.1.call-start = ((), (), s32[]{:S(2)}) async-start(), calls=%async_computation.3 | async-start | bytes 1253376 | tf_op jit(solution)/shard_map/all_gather | solution.py:95
  8.8 106.0 %all-gather.12.cloned.1.call-start = ((), (), s32[]{:S(2)}) async-start(), calls=%async_computation.4 | async-start | bytes 4456448 | tf_op jit(solution)/shard_map/all_gather | solution.py:105
  55.2 2.3 copy-start
  57.5 2.3 copy-start.1
  59.0 55.7 %copy-start.2 = (f32[64,128]{1,0:T(8,128)S(1)}, f32[64,128]{1,0:T(8,128)}, u32[]{:S(2)}) copy-start(f32[64,128]{1,0:T(8,128)} %param.10) | copy-start | bytes 98308
  59.8 111.8 %all-gather.14.cloned.1.call-start = ((), (), s32[]{:S(2)}) async-start(), calls=%async_computation.5 | async-start | bytes 2228224 | tf_op jit(solution)/shard_map/all_gather | solution.py:110
  62.3 109.3 %copy-start.3 = (f32[64]{0:T(128)S(1)}, f32[64]{0:T(128)}, u32[]{:S(2)}) copy-start(f32[64]{0:T(128)} %param.11) | copy-start | bytes 772
  119.9 115.6 %reduce-scatter.4.cloned.1.call-start = ((), (), s32[]{:S(2)}) async-start(), calls=%async_computation.6 | async-start | bytes 1253376 | tf_op jit(solution)/shard_map/reduce_scatter | solution.py:115
  180.2 176.3 %all-gather.16.cloned.1.call-start = ((), (), s32[]{:S(2)}) async-start(), calls=%async_computation.7 | async-start | bytes 1253376 | tf_op jit(solution)/shard_map/all_gather | solution.py:95
  321.4 96.9 %all-gather.18.cloned.1.call-start = ((), (), s32[]{:S(2)}) async-start(), calls=%async_computation.8 | async-start | bytes 4456448 | tf_op jit(solution)/shard_map/all_gather | solution.py:105
  363.3 111.8 %all-gather.20.cloned.1.call-start = ((), (), s32[]{:S(2)}) async-start(), calls=%async_computation.9 | async-start | bytes 2228224 | tf_op jit(solution)/shard_map/all_gather | solution.py:110
  423.4 115.6 %reduce-scatter.6.cloned.1.call-start = ((), (), s32[]{:S(2)}) async-start(), calls=%async_computation.10 | async-start | bytes 1253376 | tf_op jit(solution)/shard_map/reduce_scatter | solution.py:115
  483.7 176.1 %all-gather.22.cloned.1.call-start = ((), (), s32[]{:S(2)}) async-start(), calls=%async_computation.11 | async-start | bytes 1253376 | tf_op jit(solution)/shard_map/all_gather | solution.py:95
  624.8 96.8 %all-gather.24.cloned.1.call-start = ((), (), s32[]{:S(2)}) async-start(), calls=%async_computation.12 | async-start | bytes 4456448 | tf_op jit(solution)/shard_map/all_gather | solution.py:105
  666.7 111.8 %all-gather.26.cloned.1.call-start = ((), (), s32[]{:S(2)}) async-start(), calls=%async_computation.13 | async-start | bytes 2228224 | tf_op jit(solution)/shard_map/all_gather | solution.py:110
  726.7 115.6 %reduce-scatter.8.cloned.1.call-start = ((), (), s32[]{:S(2)}) async-start(), calls=%async_computation.14 | async-start | bytes 1253376 | tf_op jit(solution)/shard_map/reduce_scatter | solution.py:115
Sparse Core Ops, SparseCore 0:
  10.4 43.0 all-gather.9
  59.9 54.7 all-gather.11
  120.0 51.5 all-gather.13
  180.3 55.1 reduce-scatter.3
  321.5 34.8 all-gather.15
  363.4 54.7 all-gather.17
  423.5 51.5 all-gather.19
  483.8 55.1 reduce-scatter.5
  624.9 34.8 all-gather.21
  666.8 54.7 all-gather.23
  726.9 51.5 all-gather.25
  787.1 55.1 reduce-scatter.7
where the time goes:
time: 937 us; the launch traced here: 936 us
  waiting for transfers between devices  594 us (63%)
  blocking collectives  239 us (26%)
  matrix products  52.2 us (6%)
  other arithmetic  20.5 us (2%)
  between operations  14.5 us (2%)
  local copies, waits for them, and re-layouts  14.1 us (2%)
    psum x3, blocking collectives, body(): gram = lax.psum(gram_of(shaped), ('lat', 'lon'))  239 us
    reduce_scatter x3, waiting for transfers between devices, body(): lax.psum_scatter(degree_terms(spectral_grid, legendre, first).astype(jnp....  166 us
    all_gather x3, waiting for transfers between devices, body(): lax.all_gather(waves, 'lat', axis=0, tiled=True)  162 us
    all_gather x3, waiting for transfers between devices, body(): piece = lax.all_gather(scaled_grid, 'lat', axis=2, tiled=True)  152 us
    all_gather x3, waiting for transfers between devices, spread(): return lax.all_gather(block.astype(jnp.bfloat16), 'lon', axis=0, tiled=True)  114 us
  transfers between devices with their start and end apart: 12, of which 12 were waited for; matrix products, arithmetic and copies ran while one was open for 1% of the time, Pallas kernels for 0%

commit v1 on v0

v1 whole, which is shorter than its diff:
```python
import functools
import math

import jax
import jax.numpy as jnp
import numpy as np
from jax import lax
from jax.experimental import pallas as pl
from jax.experimental.pallas import tpu as pltpu
from jax.sharding import Mesh
from jax.sharding import PartitionSpec as P

T_SIZE = 1023
NLON = 2048
K = 8
STEPS = 3
NPAIR = 512
R = 1025
RP = 1152
BF = jnp.bfloat16
F32 = jnp.float32
GSCALE = 1.0 / (2.0 * NPAIR * R)
SIGNS = np.array([[1, 1, 1, 1], [1, -1, 1, -1], [1, -1, -1, 1], [1, 1, -1, -1]], np.float32)


def natural_tables():
    q = np.arange(512)[:, None]
    i2 = 2 * np.arange(512)[None, :] + 1
    out = []
    for m in (2 * q, 1023 - 2 * q):
        angle = (m * i2 % 4096) * (2.0 * math.pi / 4096)
        out += [np.cos(angle), np.sin(angle)]
    return np.stack(out).astype(jnp.bfloat16)


def fold_matrix():
    f = np.zeros((4, 4, K, 4, 4, 4, K), np.float32)
    for jj in range(4):
        for g in range(4):
            for q in range(4):
                f[jj, g, :, g, q, jj, :] = SIGNS[g, q]
    return f.reshape(128, 512)


def lanes(shape):
    return lax.broadcasted_iota(jnp.int32, shape, len(shape) - 1)


def rows(shape):
    return lax.broadcasted_iota(jnp.int32, shape, len(shape) - 2)


def split_tile(g):
    hi = g.astype(BF).astype(F32)
    rest = g - hi
    mid = rest.astype(BF).astype(F32)
    low = (rest - mid).astype(BF).astype(F32)
    return hi + pltpu.roll(mid, 8, 1) + pltpu.roll(low, 16, 1)


def join_tile(t):
    g = t + pltpu.roll(t, 120, 1) + pltpu.roll(t, 112, 1)
    lane = lanes(t.shape)
    return jnp.where((lane >= 8) & (lane < 16) & (rows(t.shape) < 8), g, 0.0)


def eliminate(gram):
    lane, row = lanes((16, 128)), rows((16, 128))
    a = jnp.where(row < 8, gram * GSCALE, jnp.where(row - 8 == lane, 1.0, 0.0))
    scale = jnp.zeros((1, 128), F32)
    lane1 = lanes((1, 128))
    for p in range(K):
        prow = a[p : p + 1, :]
        piv = jnp.sum(jnp.where(lane1 == p, prow, 0.0), axis=1, keepdims=True)
        scale = jnp.where(lane1 == p, lax.rsqrt(piv), scale)
        if p < K - 1:
            col = jnp.sum(jnp.where(lane == p, a, 0.0), axis=1, keepdims=True)
            a = a - jnp.where(lane > p, col * (prow / piv), 0.0)
    return a * scale


def even_mask(shape, pid):
    first = (lanes(shape) < T_SIZE + 1 - pid).astype(jnp.int32)
    return first != lax.rem(pid, 2)


def inverse_kernel(with_gram, pid_ref, spec_ref, leg_ref, out_ref, acc_ref):
    step = pl.program_id(0)
    per = leg_ref.shape[0]
    lane = lanes((32, 128))
    for t in range(per):
        sp = spec_ref[t // 2, 16 * (t % 2) : 16 * (t % 2) + 16, :].astype(F32)
        mask = even_mask((16, RP), pid_ref[step * per + t])
        even = jnp.where(mask, sp, 0.0).astype(BF)
        odd = jnp.where(mask, 0.0, sp).astype(BF)
        wide = jnp.concatenate([even, odd] * 4, axis=0)
        p = lax.dot_general(leg_ref[t], wide, (((1,), (1,)), ((), ())), preferred_element_type=F32)
        o = jnp.where(lane < 32, p[0:32], jnp.where(lane < 64, p[32:64], jnp.where(lane < 96, p[64:96], p[96:128])))
        acc_ref[:, step * per + t, :] = o
    if with_gram:

        @pl.when(step == 0)
        def _():
            acc_ref[:, 16:32, :] = jnp.zeros((32, 16, 128), F32)

        tile = spec_ref[0, 0:16, 1024:RP].astype(F32)
        for z in range(1, spec_ref.shape[0]):
            tile = tile + spec_ref[z, 0:16, 1024:RP].astype(F32)
        g = join_tile(tile)
        acc_ref[0, 16:32, :] += g

    @pl.when(step == pl.num_programs(0) - 1)
    def _():
        out_ref[:, 0:16, :] = acc_ref[:, 0:16, :].astype(BF)
        if with_gram:
            t = split_tile(acc_ref[0, 16:32, :]).astype(BF)
            out_ref[:, 16:32, :] = jnp.broadcast_to(t[None], (32, 16, 128))


def legendre_inverse(spec, leg, pid16, with_gram):
    height = 32 if with_gram else 16
    return pl.pallas_call(
        functools.partial(inverse_kernel, with_gram),
        grid=(4,),
        in_specs=[
            pl.BlockSpec(memory_space=pltpu.SMEM),
            pl.BlockSpec((2, 32, RP), lambda i: (i, 0, 0)),
            pl.BlockSpec((4, 128, RP), lambda i: (i, 0, 0)),
        ],
        out_specs=pl.BlockSpec((32, height, 128), lambda i: (0, 0, 0)),
        out_shape=jax.ShapeDtypeStruct((32, height, 128), BF),
        scratch_shapes=[pltpu.VMEM((32, height, 128), F32)],
        compiler_params=pltpu.CompilerParams(vmem_limit_bytes=24 << 20),
    )(pid16, spec, leg)


def grid_kernel(with_gram, x_ref, fold_ref, tt_ref, t_ref, var_ref, y_ref, hat_ref):
    x = x_ref[:, 0:16, :].reshape(512, 128)
    if with_gram:
        tile = jnp.sum(x_ref[:, 16:32, :].astype(F32), axis=0)
        gram = pltpu.roll(join_tile(tile), 120, 1)
        mix = jnp.where(lanes((8, 128)) < 8, eliminate(gram)[8:16, :], 0.0)
        for shift in (8, 16, 32, 64):
            mix = mix + pltpu.roll(mix, shift, 1)
        mix = jnp.concatenate([mix] * 16, axis=0)
    for g in range(4):
        f = fold_ref[:, 128 * g : 128 * g + 128].astype(F32)
        if with_gram:
            f = f * mix
            hi = f.astype(BF)
            low = (f - hi.astype(F32)).astype(BF)
            hat = jnp.dot(x, hi, preferred_element_type=F32) + jnp.dot(x, low, preferred_element_type=F32)
        else:
            f = jnp.where(lax.rem(rows((128, 128)), 8) == lax.rem(lanes((128, 128)), 8), f, 0.0)
            hat = jnp.dot(x, f.astype(BF), preferred_element_type=F32)
        hat_ref[512 * g : 512 * g + 512, :] = hat.astype(BF)
    grid = jnp.dot(tt_ref[...], hat_ref[...], preferred_element_type=F32)
    scaled = (grid * var_ref[...]).astype(BF)
    lane = lanes((1, 128))
    out = None
    for g in range(4):
        part = jnp.dot(t_ref[512 * g : 512 * g + 512, :], scaled, preferred_element_type=F32)
        sign = jnp.ones((1, 128), F32)
        for q in range(4):
            if SIGNS[g, q] < 0:
                sign = jnp.where((lane >= 32 * q) & (lane < 32 * q + 32), -1.0, sign)
        part = part * sign
        part = part + pltpu.roll(part, 64, 1)
        part = part + pltpu.roll(part, 32, 1)
        out = part if out is None else jnp.where(lane >= 32 * g, part, out)
    y_ref[...] = out.astype(BF).reshape(32, 16, 128)


def grid_stage(x, fold, tt, t, var, with_gram):
    return pl.pallas_call(
        functools.partial(grid_kernel, with_gram),
        out_shape=jax.ShapeDtypeStruct((32, 16, 128), BF),
        scratch_shapes=[pltpu.VMEM((2048, 128), BF)],
        compiler_params=pltpu.CompilerParams(vmem_limit_bytes=32 << 20),
    )(x, fold, tt, t, var)


def forward_kernel(pid_ref, y_ref, leg_ref, out_ref, wide_ref, lhs_ref):
    step = pl.program_id(0)
    per = leg_ref.shape[0]

    @pl.when(step == 0)
    def _():
        wide_ref[...] = y_ref[...].astype(F32)
        lane = lanes((32, 128))
        for b in range(4):
            z = jnp.concatenate([wide_ref[:, 4 * b + s, :] for s in range(4)], axis=0)
            zt = z.T
            blocks = [
                jnp.concatenate([zt[32 * g + 8 * jj : 32 * g + 8 * jj + 8, :] for g in range(4)], axis=0)
                for jj in range(4)
            ]
            for s in range(4):
                o = None
                for jj in range(4):
                    shift = (32 * (jj - s)) % 128
                    v = pltpu.roll(blocks[jj], shift, 1) if shift else blocks[jj]
                    o = v if o is None else jnp.where(lane >= 32 * jj, v, o)
                lhs_ref[4 * b + s] = o.astype(BF)

    for t in range(per):
        p = jnp.dot(lhs_ref[step * per + t], leg_ref[t], preferred_element_type=F32)
        mask = even_mask((16, RP), pid_ref[step * per + t])
        out_ref[t // 2, 16 * (t % 2) : 16 * (t % 2) + 16, :] = jnp.where(mask, p[0:16], p[16:32]).astype(BF)


def legendre_forward(y, leg, pid16):
    return pl.pallas_call(
        forward_kernel,
        grid=(4,),
        in_specs=[
            pl.BlockSpec(memory_space=pltpu.SMEM),
            pl.BlockSpec((32, 16, 128), lambda i: (0, 0, 0)),
            pl.BlockSpec((4, 128, RP), lambda i: (i, 0, 0)),
        ],
        out_specs=pl.BlockSpec((2, 32, RP), lambda i: (i, 0, 0)),
        out_shape=jax.ShapeDtypeStruct((8, 32, RP), BF),
        scratch_shapes=[pltpu.VMEM((32, 16, 128), F32), pltpu.VMEM((16, 32, 128), BF)],
        compiler_params=pltpu.CompilerParams(vmem_limit_bytes=24 << 20),
    )(pid16, y, leg)


def gram_tile(sh):
    hi = sh.astype(BF)
    low = (sh - hi.astype(F32)).astype(BF)
    both = jnp.concatenate([hi, low], axis=0)
    pad = jnp.concatenate([both, jnp.zeros((64, RP), BF)], axis=0)
    full = lax.dot_general(both, pad, (((1,), (1,)), ((), ())), preferred_element_type=F32)
    total = None
    for a in range(2):
        for b in range(2):
            for i in range(4):
                v = full[32 * a + 8 * i : 32 * a + 8 * i + 8, :]
                shift = (128 - (32 * b + 8 * i)) % 128
                v = pltpu.roll(v, shift, 1) if shift else v
                total = v if total is None else total + v
    return jnp.where(lanes((8, 128)) < 8, total, 0.0)


def summed_block(parts_ref, scale_ref):
    total = parts_ref[0].astype(F32)
    for z in range(1, parts_ref.shape[0]):
        total = total + parts_ref[z].astype(F32)
    scale = jnp.concatenate([jnp.broadcast_to(scale_ref[b : b + 1, :], (16, RP)) for b in range(2)], axis=0)
    return total * scale


def owner_kernel(parts_ref, scale_ref, weight_ref, out_ref):
    sh = summed_block(parts_ref, scale_ref)
    gram = gram_tile(sh)
    weight = jnp.concatenate([jnp.broadcast_to(weight_ref[b : b + 1, :], (16, RP)) for b in range(2)], axis=0)
    spec = (sh * weight).astype(BF)
    tile = split_tile(pltpu.roll(gram, 8, 1))
    tile = jnp.concatenate([tile, jnp.zeros((24, 128), F32)], axis=0)
    last = jnp.where(lanes((32, 128)) == 0, spec[:, 1024:RP].astype(F32), tile).astype(BF)
    for z in range(out_ref.shape[0]):
        out_ref[z, :, 0:1024] = spec[:, 0:1024]
        out_ref[z, :, 1024:RP] = last


def owner_step(parts, scale, weight):
    return pl.pallas_call(
        owner_kernel,
        out_shape=jax.ShapeDtypeStruct((8, 32, RP), BF),
        compiler_params=pltpu.CompilerParams(vmem_limit_bytes=24 << 20),
    )(parts, scale, weight)


def last_kernel(parts_ref, scale_ref, sh_ref, gram_ref):
    sh = summed_block(parts_ref, scale_ref)
    sh_ref[...] = sh
    gram_ref[...] = gram_tile(sh)


def last_step(parts, scale):
    return pl.pallas_call(
        last_kernel,
        out_shape=(jax.ShapeDtypeStruct((32, RP), F32), jax.ShapeDtypeStruct((8, 128), F32)),
        compiler_params=pltpu.CompilerParams(vmem_limit_bytes=24 << 20),
    )(parts, scale)


def finish_kernel(sh_ref, gram_ref, cos_ref, sin_ref, modes_ref, lower_ref):
    rowsum = gram_ref[0:8, :]
    for i in range(1, gram_ref.shape[0] // 8):
        rowsum = rowsum + gram_ref[8 * i : 8 * i + 8, :]
    both = eliminate(jnp.concatenate([rowsum, jnp.zeros((8, 128), F32)], axis=0))
    lower_ref[...] = jnp.where(lanes((8, 128)) <= rows((8, 128)), both[0:8, :], 0.0)
    mix = both[8:16, :]
    for b in range(2):
        cos, sin = cos_ref[b : b + 1, :], sin_ref[b : b + 1, :]
        parts = []
        for c in range(2):
            block = sh_ref[16 * b + 8 * c : 16 * b + 8 * c + 8, :]
            out = jnp.zeros((8, RP), F32)
            for q in range(K):
                coef = jnp.sum(jnp.where(rows((8, 8)) == lanes((8, 8)), jnp.broadcast_to(mix[q : q + 1, 0:8], (8, 8)), 0.0), axis=1, keepdims=True)
                out = out + coef * block[q : q + 1, :]
            parts.append(out)
        modes_ref[b, 0] = cos * parts[0] + sin * parts[1]
        modes_ref[b, 1] = sin * parts[0] - cos * parts[1]


def finish(sh, grams, cos, sin):
    return pl.pallas_call(
        finish_kernel,
        out_shape=(jax.ShapeDtypeStruct((2, 2, K, RP), F32), jax.ShapeDtypeStruct((8, 128), F32)),
        compiler_params=pltpu.CompilerParams(vmem_limit_bytes=24 << 20),
    )(sh, grams, cos, sin)


def owner_tables(pid2):
    places = jnp.arange(RP, dtype=jnp.int32)[None, :]
    pid = pid2[:, None]
    first = places < T_SIZE + 1 - pid
    degree = jnp.where(first, pid + places, places - 1)
    wave = jnp.where(first, pid, T_SIZE - pid)
    level = degree.astype(F32)
    scale = lax.rsqrt(1.0 + level * (level + 1.0) * (4.0 / (T_SIZE * T_SIZE)))
    scale = jnp.where(places < R, scale * (1.0 / NLON), 0.0)
    weight = jnp.where(wave == 0, 1.0, 2.0).astype(F32)
    phase = wave.astype(F32) * (2.0 * math.pi / (2 * NLON))
    return scale, weight, jnp.cos(phase), jnp.sin(phase)


def body(start_block, legendre, variance, gauss_weight, pair_of_slot):
    lat, zpos, core = lax.axis_index("lat"), lax.axis_index("z"), lax.axis_index("c")
    pids = pair_of_slot.reshape(16, 8, 2, 2)
    pid2 = lax.dynamic_slice(pids, (lat, zpos, core, 0), (1, 1, 1, 2)).reshape(2)
    pid16 = lax.dynamic_slice(pids, (lat, 0, core, 0), (1, 8, 1, 2)).reshape(16)
    pid_recv = pids.transpose(0, 2, 1, 3).reshape(512)

    leg = legendre.reshape(8, 2, 2, 64, R)
    other = lax.dynamic_slice_in_dim(leg, 1 - core, 1, 1)
    mine = lax.dynamic_slice_in_dim(leg, core, 1, 1)
    got = lax.ppermute(other, "c", [(0, 1), (1, 0)])
    both = jnp.where(core == 0, jnp.stack([mine, got], axis=3), jnp.stack([got, mine], axis=3))
    both = jnp.pad(both.reshape(16, 128, R), ((0, 0), (0, 0), (0, RP - R)))

    var = variance * gauss_weight[:, None]
    var = var.reshape(2, 32, 128).transpose(1, 0, 2)
    var = lax.all_to_all(var, ("lat", "c"), 0, 0, tiled=True)
    var = var.reshape(16, 4, 128).transpose(1, 0, 2).reshape(4, 4, 512)
    var = jnp.stack([var[:, 0], var[:, 1, ::-1], var[:, 2], var[:, 3, ::-1]], axis=0)
    var = jnp.repeat(var.reshape(16, 512).T, K, axis=1)

    place = jnp.where(pid_recv % 2 == 0, pid_recv, T_SIZE - pid_recv) // 2
    nat = natural_tables()
    hot = (place[:, None] == jnp.arange(512, dtype=jnp.int32)[None, :]).astype(BF)
    t = jnp.einsum("sq,gqi->gsi", hot, jnp.asarray(nat), preferred_element_type=F32).astype(BF).reshape(2048, 512)
    nat_t = np.ascontiguousarray(nat.transpose(2, 0, 1))
    tt = jnp.einsum("igq,sq->igs", jnp.asarray(nat_t), hot, preferred_element_type=F32).astype(BF).reshape(512, 2048)
    fold = jnp.asarray(fold_matrix(), BF)

    scale, weight, cos, sin = owner_tables(pid2)
    start = jnp.pad(start_block, ((0, 0), (0, 0), (0, 0), (0, RP - R)))
    re, im = start[:, :, 0, :], start[:, :, 1, :]
    cb, sb, wb = cos[:, None, :], sin[:, None, :], weight[:, None, :]
    spec = jnp.stack([wb * (re * cb + im * sb), wb * (re * sb - im * cb)], axis=1).astype(BF)
    spec = jnp.broadcast_to(spec.reshape(1, 32, RP), (8, 32, RP))

    for step in range(STEPS):
        spec = lax.all_to_all(spec, "z", 0, 0, tiled=True)
        x = legendre_inverse(spec, both, pid16, step > 0)
        x = lax.all_to_all(x, ("lat", "c"), 0, 0, tiled=True)
        y = grid_stage(x, fold, tt, t, var, step > 0)
        y = lax.all_to_all(y, ("lat", "c"), 0, 0, tiled=True)
        parts = legendre_forward(y, both, pid16)
        parts = lax.all_to_all(parts, "z", 0, 0, tiled=True)
        if step + 1 < STEPS:
            spec = owner_step(parts, scale, weight)
    sh, gram = last_step(parts, scale)
    grams = lax.all_to_all(jnp.broadcast_to(gram[None, :, 0:8].reshape(1, 64), (256, 64)), ("lat", "z", "c"), 0, 0, tiled=True)
    total = jnp.sum(grams, axis=0).reshape(8, 8)
    modes, lower = finish(sh, jnp.pad(total, ((0, 0), (0, 120))), cos, sin)
    return modes.transpose(0, 2, 1, 3)[:, :, :, :R], lower[:, :K]


def solution(mesh):
    fine = Mesh(mesh.devices.reshape(16, 8, 2), ("lat", "z", "c"))
    placed = (
        P(("lat", "z", "c"), None, None, None),
        P("lat", ("z", "c"), None),
        P(("z", "c"), "lat"),
        P(("z", "c")),
        P(),
    )
    return jax.shard_map(
        body,
        mesh=fine,
        in_specs=placed,
        out_specs=(P(("lat", "z", "c"), None, None, None), P()),
        check_vma=False,
    )
```

time: 937 us -> 291 us (0.31)
  waiting for transfers between devices: 594 us -> 17.8 us
  blocking collectives: 239 us -> 186 us
  matrix products: 52.2 us -> 7.07 us
  Pallas kernels: 0 us -> 29.6 us
  starting transfers between devices: 1.16 us -> 24.4 us
  other arithmetic: 20.5 us -> 6.41 us
  between operations: 14.5 us -> 0.96 us
    all_gather x9 -> x0, waiting for transfers between devices: 428 us -> none  [the longest x3 162 us: body(): lax.all_gather(waves, 'lat', axis=0, tiled=True)]
    psum x3 -> x0, blocking collectives: 239 us -> none  [body(): gram = lax.psum(gram_of(shaped), ('lat', 'lon'))]
    all_to_all x0 -> x11, blocking collectives: none -> 186 us  [the longest x3 63.5 us: body(): parts = lax.all_to_all(parts, 'z', 0, 0, tiled=True)]
    reduce_scatter x3 -> x0, waiting for transfers between devices: 166 us -> none  [body(): lax.psum_scatter(degree_terms(spectral_grid, legendre, first).astype(jnp....]
    dot_general x18 -> x2, matrix products: 51.6 us -> 7.07 us  [the longest x1 4.36 us: body(): jnp.einsum('igq,sq->igs', jnp.asarray(nat_t), hot, preferred_element_type...]
    pallas_call x0 -> x13, Pallas kernels: none -> 29.6 us  [the longest x3 10.6 us: grid_stage(): pl.pallas_call(functools.partial(grid_kernel, with_gram), out_shape=jax.S...]
    all_to_all x0 -> x3, starting transfers between devices: none -> 21.1 us  [the longest x1 8.19 us: body(): spec = lax.all_to_all(spec, 'z', 0, 0, tiled=True)]
    all_to_all x0 -> x3, waiting for transfers between devices: none -> 17.8 us  [the longest x1 10.3 us: body(): spec = lax.all_to_all(spec, 'z', 0, 0, tiled=True)]
  transfers between devices with their start and end apart: 12 -> 4, of which waited for: 12 -> 2; matrix products, arithmetic and copies ran while one was open for 1% -> 7% of each run, Pallas kernels for 0% -> 0%
where the time goes in v1:
time: 291 us; the launch traced here: 290 us
  blocking collectives  186 us (64%)
  Pallas kernels  29.6 us (10%)
  starting transfers between devices  24.4 us (8%)
  local copies, waits for them, and re-layouts  18.4 us (6%)
  waiting for transfers between devices  17.8 us (6%)
  matrix products  7.07 us (2%)
  other arithmetic  6.41 us (2%)
    all_to_all x3, blocking collectives, body(): parts = lax.all_to_all(parts, 'z', 0, 0, tiled=True)  63.5 us
    all_to_all x2, blocking collectives, body(): spec = lax.all_to_all(spec, 'z', 0, 0, tiled=True)  39.4 us
    all_to_all x3, blocking collectives, body(): y = lax.all_to_all(y, ('lat', 'c'), 0, 0, tiled=True)  33.6 us
    all_to_all x2, blocking collectives, body(): x = lax.all_to_all(x, ('lat', 'c'), 0, 0, tiled=True)  30.2 us
    all_to_all x1, blocking collectives, body(): lax.all_to_all(jnp.broadcast_to(gram[None, :, 0:8].reshape(1, 64), (256,...  18.8 us
    pallas_call x3, Pallas kernels, grid_stage(): pl.pallas_call(functools.partial(grid_kernel, with_gram), out_shape=jax.S...  10.6 us
    all_to_all x1, waiting for transfers between devices, body(): spec = lax.all_to_all(spec, 'z', 0, 0, tiled=True)  10.3 us
    pallas_call x3, Pallas kernels, legendre_inverse(): pl.pallas_call(functools.partial(inverse_kernel, with_gram), grid=(4,), i...  9.84 us
  transfers between devices with their start and end apart: 4, of which 2 were waited for; matrix products, arithmetic and copies ran while one was open for 7% of the time, Pallas kernels for 0%

profile of v1, /device:TPU:1, one launch (start us, length us, event | category | flops | bytes accessed | tf_op | source)
XLA Modules:
  0.0 290.3 jit_solution(5826968331127539065)
XLA Ops:
  0.6 0.0 copy-start.5
  0.6 0.0 copy-start.7
  0.7 0.0 copy-start.6
  0.7 0.0 copy-start.4
  0.7 5.1 %dynamic-slice_bitcast_fusion.1 = (bf16[8,1,2,1,64,1025]{5,4,3,2,0,1:T(8,128)(2,1)}, bf16[8,1,2,64,1025]{4,3,2,0,1:T(8,128)(2,1)}) fusion(bf16[8,2,2,64,1025]{4,3,2,1,0:T(8,128)(2,1)} %bitcast.69, s32[]{:T(128)S(6)} %select_n.83, s32[]{:T(128)S(6)} %select_n.88), kind=kLoop, calls=%fused_computation.2 | loop fusion | bytes 8396808 | tf_op jit(solution)/shard_map/stack | solution.py:342
  5.8 3.2 %collective-permute-start = (bf16[8,1,2,64,1025]{4,3,2,0,1:T(8,128)(2,1)}, bf16[8,1,2,64,1025]{4,3,2,0,1:T(8,128)(2,1)}, u32[]{:S(2)}, u32[]{:S(2)}) collective-permute-start(bf16[8,1,2,64,1025]{4,3,2,0,1:T(8,128)(2,1)} %get-tuple-element.21), channel_id=1, source_target_pairs={{0,1},{1,0},{2,3},{3,2},{4,5},{5,4},{6,7},{7,6},{8,9},{9,8},{10,11... | collective-permute-start | bytes 6297608 | tf_op jit(solution)/shard_map/ppermute | solution.py:341
  9.0 0.0 copy-done.5
  9.0 0.0 copy-done.7
  9.0 0.1 broadcast_multiply_fusion
  9.1 0.6 copy.54
  9.8 5.5 %all-to-all-start.2 = ((f32[32,2,128]{2,1,0:T(2,128)}), f32[32,2,128]{2,1,0:T(2,128)S(1)}, u32[]{:S(2)}, u32[]{:S(2)}) async-start(f32[32,2,128]{2,1,0:T(2,128)} %bitcast.59), calls=%async_computation.2 | async-start | bytes 65536 | tf_op jit(solution)/shard_map/all_to_all | solution.py:347
  15.3 0.2 reshape.326
  15.6 0.1 reshape.329
  15.7 0.0 copy-start.8
  15.8 4.4 %convolution_convert_fusion.1 = bf16[512,512,4]{1,0,2:T(8,128)(2,1)} fusion(bf16[512,4,512]{2,0,1:T(8,128)(2,1)} %constant.81.clone, s32[512]{0:T(512)S(1)} %add_select_fusion), kind=kOutput, calls=%fused_computation.4 | convolution fusion | flops 1075052544 | bytes 4196352 | tf_op jit(solution)/shard_map/igq,sq->igs/dot_general | solution.py:357
  20.1 0.0 copy-done.8
  20.1 2.7 convolution_convert_fusion
  22.8 0.2 compare_select_fusion
  23.2 0.1 reshape.327.pid_ref
  23.2 2.9 %copy.50.tt_ref = bf16[512,2048]{1,0:T(8,128)(2,1)S(1)} copy(bf16[512,2048]{0,1:T(8,128)(2,1)} %bitcast.70) | data formatting | bytes 4194304 | tf_op jit(solution)/shard_map/reshape | solution.py:357
  26.2 0.0 all-to-all-done.2
  26.2 0.8 broadcast_in_dim.70
  27.0 8.2 %all-to-all-start = ((bf16[8,32,1152]{2,1,0:T(8,128)(2,1)}), bf16[8,32,1152]{2,1,0:T(8,128)(2,1)S(1)}, u32[]{:S(2)}, u32[]{:S(2)}) async-start(bf16[8,32,1152]{2,1,0:T(8,128)(2,1)} %broadcast_in_dim.70), calls=%async_computation | async-start | bytes 1179648 | tf_op jit(solution)/shard_map/all_to_all | solution.py:368
  35.2 0.4 rev.6
  35.6 0.4 rev.7
  36.0 0.0 collective-permute-done
  36.0 5.7 %maximum_select_fusion = bf16[8,1,2,2,64,1025]{5,4,3,2,0,1:T(8,128)(2,1)S(1)} fusion(bf16[8,1,2,1,64,1025]{5,4,3,2,0,1:T(8,128)(2,1)} %bitcast.8, bf16[8,1,2,1,64,1025]{5,4,3,2,0,1:T(8,128)(2,1)} %get-tuple-element.20, pred[]{:T(512)S(6)} %eq.38), kind=kLoop, calls=%fused_computation | loop fusion | flops 6297600 | bytes 8396801 | tf_op jit(solution)/shard_map/jit(_where)/select_n | solution.py:342
  41.7 2.6 pad.13.leg_ref
  44.3 10.3 %all-to-all-done.spec_ref = bf16[8,32,1152]{2,1,0:T(8,128)(2,1)S(1)} async-done(((bf16[8,32,1152]{2,1,0:T(8,128)(2,1)}), bf16[8,32,1152]{2,1,0:T(8,128)(2,1)S(1)}, u32[]{:S(2)}, u32[]{:S(2)}) %all-to-all-start) | async-done | bytes 589856 | tf_op jit(solution)/shard_map/all_to_all | solution.py:368
  54.6 2.3 copy-done
  56.9 3.4 %shard_map.95 = bf16[32,16,128]{2,1,0:T(8,128)(2,1)} custom-call(s32[16]{0:T(128)S(1)} %reshape.327.pid_ref, bf16[8,32,1152]{2,1,0:T(8,128)(2,1)S(1)} %all-to-all-done.spec_ref, bf16[16,128,1152]{2,1,0:T(8,128)(2,1)S(1)} %copy-done), custom_call_target="tpu_custom_call" | custom-call | tf_op jit(solution)/shard_map/pallas_call | solution.py:122
  60.4 7.5 %all-to-all-start.1 = ((bf16[32,16,128]{2,1,0:T(8,128)(2,1)}), bf16[32,16,128]{2,1,0:T(8,128)(2,1)S(1)}, u32[]{:S(2)}, u32[]{:S(2)}) async-start(bf16[32,16,128]{2,1,0:T(8,128)(2,1)} %shard_map.95), calls=%async_computation.1 | async-start | bytes 262144 | tf_op jit(solution)/shard_map/all_to_all | solution.py:370
  67.9 0.1 copy.45.var_ref
  68.0 7.5 %all-to-all-done.1.x_ref = bf16[32,16,128]{2,1,0:T(8,128)(2,1)S(1)} async-done(((bf16[32,16,128]{2,1,0:T(8,128)(2,1)}), bf16[32,16,128]{2,1,0:T(8,128)(2,1)S(1)}, u32[]{:S(2)}, u32[]{:S(2)}) %all-to-all-start.1) | async-done | bytes 131104 | tf_op jit(solution)/shard_map/all_to_all | solution.py:370
  75.6 1.6 copy-done.2
  77.2 2.7 shard_map.96
  79.9 11.3 %all_to_all.71.y_ref = bf16[32,16,128]{2,1,0:T(8,128)(2,1)S(1)} all-to-all(bf16[32,16,128]{2,1,0:T(8,128)(2,1)S(1)} %shard_map.96), channel_id=1, replica_groups=mesh['lat'=16,'z'=8,'c'=2] {'lat','c'}, dimensions={0} | all-to-all | bytes 262144 | tf_op jit(solution)/shard_map/all_to_all | solution.py:372
  91.2 0.0 copy-done.1
  91.2 2.2 shard_map.97
  93.4 21.2 %all_to_all.72.parts_ref = bf16[8,32,1152]{2,1,0:T(8,128)(2,1)S(1)} all-to-all(bf16[8,32,1152]{2,1,0:T(8,128)(2,1)S(1)} %shard_map.97), channel_id=1, replica_groups=mesh['lat'=16,'z'=8,'c'=2] {'z'}, dimensions={0} | all-to-all | bytes 1179648 | tf_op jit(solution)/shard_map/all_to_all | solution.py:374
  114.6 0.5 shard_map.98
  115.0 19.7 %all_to_all.73.spec_ref = bf16[8,32,1152]{2,1,0:T(8,128)(2,1)S(1)} all-to-all(bf16[8,32,1152]{2,1,0:T(8,128)(2,1)S(1)} %shard_map.98), channel_id=1, replica_groups=mesh['lat'=16,'z'=8,'c'=2] {'z'}, dimensions={0} | all-to-all | bytes 1179648 | tf_op jit(solution)/shard_map/all_to_all | solution.py:368
  134.7 3.2 %shard_map.99 = bf16[32,32,128]{2,1,0:T(8,128)(2,1)S(1)} custom-call(s32[16]{0:T(128)S(1)} %reshape.327.pid_ref, bf16[8,32,1152]{2,1,0:T(8,128)(2,1)S(1)} %all_to_all.73.spec_ref, bf16[16,128,1152]{2,1,0:T(8,128)(2,1)S(1)} %copy-done.1), custom_call_target="tpu_custom_call" | custom-call | tf_op jit(solution)/shard_map/pallas_call | solution.py:122
  137.9 15.1 %all_to_all.74.x_ref = bf16[32,32,128]{2,1,0:T(8,128)(2,1)S(1)} all-to-all(bf16[32,32,128]{2,1,0:T(8,128)(2,1)S(1)} %shard_map.99), channel_id=1, replica_groups=mesh['lat'=16,'z'=8,'c'=2] {'lat','c'}, dimensions={0} | all-to-all | bytes 524288 | tf_op jit(solution)/shard_map/all_to_all | solution.py:370
  153.0 3.9 %shard_map.100 = bf16[32,16,128]{2,1,0:T(8,128)(2,1)S(1)} custom-call(bf16[32,32,128]{2,1,0:T(8,128)(2,1)S(1)} %all_to_all.74.x_ref, bf16[128,512]{1,0:T(8,128)(2,1)S(1)} %copy-done.3, bf16[512,2048]{1,0:T(8,128)(2,1)S(1)} %copy.50.tt_ref, bf16[2048,512]{1,0:T(8,128)(2,1)S(1)} %bitcast.64, f32[512,128]{1,0:T(8,128)S(1)} %copy.45.var_ref), custom_call_target="tpu_custom_call" | custom-call | tf_op jit(solution)/shard_map/pallas_call | solution.py:175
  157.0 11.2 %all_to_all.75.y_ref = bf16[32,16,128]{2,1,0:T(8,128)(2,1)S(1)} all-to-all(bf16[32,16,128]{2,1,0:T(8,128)(2,1)S(1)} %shard_map.100), channel_id=1, replica_groups=mesh['lat'=16,'z'=8,'c'=2] {'lat','c'}, dimensions={0} | all-to-all | bytes 262144 | tf_op jit(solution)/shard_map/all_to_all | solution.py:372
  168.1 2.2 shard_map.101
  170.4 21.2 %all_to_all.76.parts_ref = bf16[8,32,1152]{2,1,0:T(8,128)(2,1)S(1)} all-to-all(bf16[8,32,1152]{2,1,0:T(8,128)(2,1)S(1)} %shard_map.101), channel_id=1, replica_groups=mesh['lat'=16,'z'=8,'c'=2] {'z'}, dimensions={0} | all-to-all | bytes 1179648 | tf_op jit(solution)/shard_map/all_to_all | solution.py:374
  191.5 0.5 shard_map.102
  192.0 19.7 %all_to_all.77.spec_ref = bf16[8,32,1152]{2,1,0:T(8,128)(2,1)S(1)} all-to-all(bf16[8,32,1152]{2,1,0:T(8,128)(2,1)S(1)} %shard_map.102), channel_id=1, replica_groups=mesh['lat'=16,'z'=8,'c'=2] {'z'}, dimensions={0} | all-to-all | bytes 1179648 | tf_op jit(solution)/shard_map/all_to_all | solution.py:368
  211.7 3.2 %shard_map.103 = bf16[32,32,128]{2,1,0:T(8,128)(2,1)S(1)} custom-call(s32[16]{0:T(128)S(1)} %reshape.327.pid_ref, bf16[8,32,1152]{2,1,0:T(8,128)(2,1)S(1)} %all_to_all.77.spec_ref, bf16[16,128,1152]{2,1,0:T(8,128)(2,1)S(1)} %copy-done.1), custom_call_target="tpu_custom_call" | custom-call | tf_op jit(solution)/shard_map/pallas_call | solution.py:122
  214.9 15.1 %all_to_all.78.x_ref = bf16[32,32,128]{2,1,0:T(8,128)(2,1)S(1)} all-to-all(bf16[32,32,128]{2,1,0:T(8,128)(2,1)S(1)} %shard_map.103), channel_id=1, replica_groups=mesh['lat'=16,'z'=8,'c'=2] {'lat','c'}, dimensions={0} | all-to-all | bytes 524288 | tf_op jit(solution)/shard_map/all_to_all | solution.py:370
  230.0 3.9 %shard_map.104 = bf16[32,16,128]{2,1,0:T(8,128)(2,1)S(1)} custom-call(bf16[32,32,128]{2,1,0:T(8,128)(2,1)S(1)} %all_to_all.78.x_ref, bf16[128,512]{1,0:T(8,128)(2,1)S(1)} %copy-done.3, bf16[512,2048]{1,0:T(8,128)(2,1)S(1)} %copy.50.tt_ref, bf16[2048,512]{1,0:T(8,128)(2,1)S(1)} %bitcast.65, f32[512,128]{1,0:T(8,128)S(1)} %copy.45.var_ref), custom_call_target="tpu_custom_call" | custom-call | tf_op jit(solution)/shard_map/pallas_call | solution.py:175
  233.9 11.2 %all_to_all.79.y_ref = bf16[32,16,128]{2,1,0:T(8,128)(2,1)S(1)} all-to-all(bf16[32,16,128]{2,1,0:T(8,128)(2,1)S(1)} %shard_map.104), channel_id=1, replica_groups=mesh['lat'=16,'z'=8,'c'=2] {'lat','c'}, dimensions={0} | all-to-all | bytes 262144 | tf_op jit(solution)/shard_map/all_to_all | solution.py:372
  245.1 2.2 shard_map.105
  247.3 21.2 %all_to_all.80.parts_ref = bf16[8,32,1152]{2,1,0:T(8,128)(2,1)S(1)} all-to-all(bf16[8,32,1152]{2,1,0:T(8,128)(2,1)S(1)} %shard_map.105), channel_id=1, replica_groups=mesh['lat'=16,'z'=8,'c'=2] {'z'}, dimensions={0} | all-to-all | bytes 1179648 | tf_op jit(solution)/shard_map/all_to_all | solution.py:374
  268.5 0.3 shard_map.106
  268.8 0.1 broadcast_in_dim.75
  268.9 0.1 broadcast_in_dim.76
  269.0 18.8 %all_to_all.81 = f32[256,1,64]{2,1,0:T(1,128)S(1)} all-to-all(f32[256,1,64]{2,1,0:T(1,128)S(1)} %broadcast_in_dim.76), channel_id=1, replica_groups=mesh['lat'=16,'z'=8,'c'=2] {'lat','z','c'}, dimensions={0} | all-to-all | bytes 131072 | tf_op jit(solution)/shard_map/all_to_all | solution.py:378
  287.8 0.3 reduce_sum.9
  288.1 0.1 reshape.337
  288.2 1.3 shard_map.107
  289.5 0.7 copy.49
  (22 shorter events, 0.2 us)
Async XLA Ops:
  0.6 8.4 %copy-start.5 = (f32[64,128]{1,0:T(8,128)S(1)}, f32[64,128]{1,0:T(8,128)}, u32[]{:S(2)}) copy-start(f32[64,128]{1,0:T(8,128)} %param.10) | copy-start | bytes 98308
  0.6 8.4 %copy-start.7 = (f32[64]{0:T(128)S(1)}, f32[64]{0:T(128)}, u32[]{:S(2)}) copy-start(f32[64]{0:T(128)} %param.11) | copy-start | bytes 772
  0.7 14.6 %copy-start.6 = (s32[512]{0:T(512)S(1)}, s32[512]{0:T(512)}, u32[]{:S(2)}) copy-start(s32[512]{0:T(512)} %param.12) | copy-start | bytes 6148
  0.7 14.9 %copy-start.4 = (f32[2,8,2,1025]{3,2,1,0:T(2,128)S(1)}, f32[2,8,2,1025]{3,2,1,0:T(2,128)}, u32[]{:S(2)}) copy-start(f32[2,8,2,1025]{3,2,1,0:T(2,128)} %param.8) | copy-start | bytes 393604
  5.8 30.2 %collective-permute-start = (bf16[8,1,2,64,1025]{4,3,2,0,1:T(8,128)(2,1)}, bf16[8,1,2,64,1025]{4,3,2,0,1:T(8,128)(2,1)}, u32[]{:S(2)}, u32[]{:S(2)}) collective-permute-start(bf16[8,1,2,64,1025]{4,3,2,0,1:T(8,128)(2,1)} %get-tuple-element.21), channel_id=1, source_target_pairs={{0,1},{1,0},{2,3},{3,2},{4,5},{5,4},{6,7},{7,6},{8,9},{9,8},{10,11... | collective-permute-start | bytes 6297608 | tf_op jit(solution)/shard_map/ppermute | solution.py:341
  9.8 16.4 %all-to-all-start.2 = ((f32[32,2,128]{2,1,0:T(2,128)}), f32[32,2,128]{2,1,0:T(2,128)S(1)}, u32[]{:S(2)}, u32[]{:S(2)}) async-start(f32[32,2,128]{2,1,0:T(2,128)} %bitcast.59), calls=%async_computation.2 | async-start | bytes 65536 | tf_op jit(solution)/shard_map/all_to_all | solution.py:347
  15.7 4.4 %copy-start.8 = (bf16[4,512,512]{2,1,0:T(8,128)(2,1)S(1)}, bf16[4,512,512]{2,1,0:T(8,128)(2,1)}, u32[]{:S(2)}) copy-start(bf16[4,512,512]{2,1,0:T(8,128)(2,1)} %constant.80.clone) | copy-start | bytes 6291460
  27.0 27.6 %all-to-all-start = ((bf16[8,32,1152]{2,1,0:T(8,128)(2,1)}), bf16[8,32,1152]{2,1,0:T(8,128)(2,1)S(1)}, u32[]{:S(2)}, u32[]{:S(2)}) async-start(bf16[8,32,1152]{2,1,0:T(8,128)(2,1)} %broadcast_in_dim.70), calls=%async_computation | async-start | bytes 1179648 | tf_op jit(solution)/shard_map/all_to_all | solution.py:368
  54.6 2.3 copy-start
  56.9 18.6 %copy-start.3 = (bf16[128,512]{1,0:T(8,128)(2,1)S(1)}, bf16[128,512]{1,0:T(8,128)(2,1)}, u32[]{:S(2)}) copy-start(bf16[128,512]{1,0:T(8,128)(2,1)} %constant.82.clone.fold_ref) | copy-start | bytes 393220
  60.4 15.2 %all-to-all-start.1 = ((bf16[32,16,128]{2,1,0:T(8,128)(2,1)}), bf16[32,16,128]{2,1,0:T(8,128)(2,1)S(1)}, u32[]{:S(2)}, u32[]{:S(2)}) async-start(bf16[32,16,128]{2,1,0:T(8,128)(2,1)} %shard_map.95), calls=%async_computation.1 | async-start | bytes 262144 | tf_op jit(solution)/shard_map/all_to_all | solution.py:370
  75.6 1.6 copy-start.2
  77.2 14.0 %copy-start.1 = (bf16[16,128,1152]{2,1,0:T(8,128)(2,1)S(1)}, bf16[16,128,1152]{2,1,0:T(8,128)(2,1)}, u32[]{:S(2)}) copy-start(bf16[16,128,1152]{2,1,0:T(8,128)(2,1)} %pad.13.leg_ref) | copy-start | bytes 14155780

commit v2 on v0

v2 whole, which is shorter than its diff:
```python
import functools
import math

import jax
import jax.numpy as jnp
import numpy as np
from jax import lax
from jax.experimental import pallas as pl
from jax.experimental.pallas import tpu as pltpu
from jax.sharding import Mesh
from jax.sharding import PartitionSpec as P

T_SIZE = 1023
NLON = 2048
K = 8
STEPS = 3
NPAIR = 512
R = 1025
RP = 1152
BF = jnp.bfloat16
F32 = jnp.float32
GSCALE = 1.0 / (2.0 * NPAIR * R)
SIGNS = np.array([[1, 1, 1, 1], [1, -1, 1, -1], [1, -1, -1, 1], [1, 1, -1, -1]], np.float32)


def natural_tables():
    q = np.arange(512)[:, None]
    i2 = 2 * np.arange(512)[None, :] + 1
    out = []
    for m in (2 * q, 1023 - 2 * q):
        angle = (m * i2 % 4096) * (2.0 * math.pi / 4096)
        out += [np.cos(angle), np.sin(angle)]
    return np.stack(out).astype(jnp.bfloat16)


def fold_matrix():
    f = np.zeros((4, 4, K, 4, 4, 4, K), np.float32)
    for jj in range(4):
        for g in range(4):
            for q in range(4):
                f[jj, g, :, g, q, jj, :] = SIGNS[g, q]
    return f.reshape(128, 512)


def lanes(shape):
    return lax.broadcasted_iota(jnp.int32, shape, len(shape) - 1)


def rows(shape):
    return lax.broadcasted_iota(jnp.int32, shape, len(shape) - 2)


def split_tile(g):
    hi = g.astype(BF).astype(F32)
    rest = g - hi
    mid = rest.astype(BF).astype(F32)
    low = (rest - mid).astype(BF).astype(F32)
    return hi + pltpu.roll(mid, 8, 1) + pltpu.roll(low, 16, 1)


def join_tile(t):
    g = t + pltpu.roll(t, 120, 1) + pltpu.roll(t, 112, 1)
    lane = lanes(t.shape)
    return jnp.where((lane >= 8) & (lane < 16) & (rows(t.shape) < 8), g, 0.0)


def splat_factor(gram):
    g = [[jnp.broadcast_to(gram[i : i + 1, j : j + 1] * GSCALE, (8, 128)) for j in range(i + 1)] for i in range(K)]
    low = [[None] * K for _ in range(K)]
    inv = [[None] * K for _ in range(K)]
    for j in range(K):
        d = g[j][j]
        for p in range(j):
            d = d - low[j][p] * low[j][p]
        r = lax.rsqrt(d)
        r = r * (1.5 - 0.5 * d * r * r)
        low[j][j] = d * r
        inv[j][j] = r
        for i in range(j + 1, K):
            v = g[i][j]
            for p in range(j):
                v = v - low[i][p] * low[j][p]
            low[i][j] = v * r
    for j in range(K):
        for i in range(j + 1, K):
            v = low[i][j] * inv[j][j]
            for p in range(j + 1, i):
                v = v + low[i][p] * inv[p][j]
            inv[i][j] = -(v * inv[i][i])
    return low, inv


def tile_of(entries, transposed, period):
    row, lane = rows((8, 128)), lanes((8, 128))
    if period:
        lane = lax.rem(lane, period)
    out = jnp.zeros((8, 128), F32)
    for i in range(K):
        for j in range(i + 1):
            r, l = (j, i) if transposed else (i, j)
            out = jnp.where((row == r) & (lane == l), entries[i][j], out)
    return out


def even_mask(shape, pid):
    first = (lanes(shape) < T_SIZE + 1 - pid).astype(jnp.int32)
    return first != lax.rem(pid, 2)


def load_block(ref, z, b):
    main = [ref[z, (b * 8 + l) * 16 : (b * 8 + l) * 16 + 16, :].astype(F32) for l in range(8)]
    extra = ref[z, 256:272, :].astype(F32)
    if b:
        extra = pltpu.roll(extra, 128 - b, 1)
    return jnp.concatenate(main + [jnp.where(lanes((16, 128)) == 0, extra, 0.0)], axis=1)


def pack(blocks, tile):
    lane = lanes((16, 128))
    pieces = [v[:, 128 * l : 128 * l + 128].astype(BF) for v in blocks for l in range(8)]
    extra = jnp.where(lane == 0, blocks[0][:, 1024:RP], jnp.where(lane == 1, pltpu.roll(blocks[1][:, 1024:RP], 1, 1), tile))
    return pieces + [extra.astype(BF)]


def start_kernel(pid_ref, at_ref, start_ref, out_ref, table_ref):
    base = at_ref[0] + at_ref[1]
    place, row = lanes((2, RP)), rows((2, RP))
    pid = jnp.where(row == 0, pid_ref[base], pid_ref[base + 1])
    first = place < T_SIZE + 1 - pid
    degree = jnp.where(first, pid + place, place - 1)
    wave = jnp.where(first, pid, T_SIZE - pid)
    level = degree.astype(F32)
    scale = lax.rsqrt(1.0 + level * (level + 1.0) * (4.0 / (T_SIZE * T_SIZE)))
    scale = jnp.where(place < R, scale * (1.0 / NLON), 0.0)
    weight = jnp.where(wave == 0, 1.0, 2.0).astype(F32)
    phase = wave.astype(F32) * (2.0 * math.pi / (2 * NLON))
    cos, sin = jnp.cos(phase), jnp.sin(phase)
    table_ref[0:2, :] = scale
    table_ref[2:4, :] = weight
    table_ref[4:6, :] = cos
    table_ref[6:8, :] = sin
    lane = lanes((8, 128))
    blocks = []
    for b in range(2):
        half = []
        for c in range(2):
            col = jnp.broadcast_to(start_ref[b, :, c, 1024:R], (8, 128))
            half.append(jnp.concatenate([start_ref[b, :, c, 0:1024], jnp.where(lane == 0, col, 0.0)], axis=1))
        re, im = half
        cb, sb, wb = cos[b : b + 1], sin[b : b + 1], weight[b : b + 1]
        blocks.append(jnp.concatenate([wb * (re * cb + im * sb), wb * (re * sb - im * cb)], axis=0))
    pieces = pack(blocks, jnp.zeros((16, 128), F32))
    for z in range(out_ref.shape[0]):
        for n, v in enumerate(pieces):
            out_ref[z, 16 * n : 16 * n + 16, :] = v


SMEM = pl.BlockSpec(memory_space=pltpu.SMEM)
VMEM = pl.BlockSpec(memory_space=pltpu.VMEM)


def start_step(pids, at, start):
    return pl.pallas_call(
        start_kernel,
        in_specs=[SMEM, SMEM, VMEM],
        out_shape=(jax.ShapeDtypeStruct((8, 272, 128), BF), jax.ShapeDtypeStruct((8, RP), F32)),
        compiler_params=pltpu.CompilerParams(vmem_limit_bytes=12 << 20),
    )(pids, at, start)


def table_kernel(place_ref, nat_ref, natt_ref, t_ref, tt_ref):
    hot = jnp.where(rows((512, 512)) == place_ref[...], 1.0, 0.0)
    hot_s = hot.T.astype(BF)
    hot = hot.astype(BF)
    for g in range(4):
        t_ref[512 * g : 512 * g + 512, :] = jnp.dot(hot_s, nat_ref[512 * g : 512 * g + 512, :], preferred_element_type=F32).astype(BF)
        tt_ref[:, 512 * g : 512 * g + 512] = jnp.dot(natt_ref[:, 512 * g : 512 * g + 512], hot, preferred_element_type=F32).astype(BF)


def slot_tables(place):
    nat = natural_tables()
    natt = np.ascontiguousarray(nat.transpose(2, 0, 1)).reshape(512, 2048)
    return pl.pallas_call(
        table_kernel,
        out_shape=(jax.ShapeDtypeStruct((2048, 512), BF), jax.ShapeDtypeStruct((512, 2048), BF)),
        compiler_params=pltpu.CompilerParams(vmem_limit_bytes=12 << 20),
    )(place, jnp.asarray(nat.reshape(2048, 512)), jnp.asarray(natt))


def slot_waves(spec_ref, z, b, pid, leg):
    lane = lanes((32, 128))
    sp = load_block(spec_ref, z, b)
    mask = even_mask((16, RP), pid)
    even = jnp.where(mask, sp, 0.0).astype(BF)
    odd = jnp.where(mask, 0.0, sp).astype(BF)
    wide = jnp.concatenate([even, odd] * 4, axis=0)
    p = lax.dot_general(leg, wide, (((1,), (1,)), ((), ())), preferred_element_type=F32)
    return jnp.where(lane < 32, p[0:32], jnp.where(lane < 64, p[32:64], jnp.where(lane < 96, p[64:96], p[96:128])))


def combine_kernel(at_ref, leg_ref, got_ref, both_ref):
    core = at_ref[2]
    lane = lanes((64, 128))
    for b in range(2):
        for ref, half in ((leg_ref, core), (got_ref, 1 - core)):
            at = pl.ds(pl.multiple_of(half * 64, 64), 64)
            both_ref[b, at, 0:1024] = ref[b, :, 0:1024]
            col = jnp.broadcast_to(ref[b, :, 1024:R].astype(F32), (64, 128))
            both_ref[b, at, 1024:RP] = jnp.where(lane == 0, col, 0.0).astype(BF)


def combine(at, leg, got):
    return pl.pallas_call(
        combine_kernel,
        grid_spec=pltpu.PrefetchScalarGridSpec(
            num_scalar_prefetch=1,
            grid=(8,),
            in_specs=[pl.BlockSpec((2, 64, R), lambda i, at: (2 * i + at[2], 0, 0))] * 2,
            out_specs=pl.BlockSpec((2, 128, RP), lambda i, at: (i, 0, 0)),
        ),
        out_shape=jax.ShapeDtypeStruct((16, 128, RP), BF),
        compiler_params=pltpu.CompilerParams(vmem_limit_bytes=8 << 20),
    )(at, leg, got)


def inverse_kernel(first, pid_ref, at_ref, spec_ref, leg_ref, *refs):
    if first:
        var_ref, gauss_ref, out_ref, acc_ref = refs
        acc_ref[:, 16:32, :] = jnp.zeros((32, 16, 128), F32)
        gauss = jnp.broadcast_to(gauss_ref[...], (64, 64))
        gauss = jnp.sum(jnp.where(rows((64, 64)) == lanes((64, 64)), gauss, 0.0), axis=1, keepdims=True)
        rest = var_ref[...] * gauss
        for n in range(3):
            term = rest.astype(BF).astype(F32)
            rest = rest - term
            for jh in range(2):
                acc_ref[:, 16 + 2 * n + jh, :] = term[32 * jh : 32 * jh + 32, :]
    else:
        out_ref, acc_ref = refs
        tile = spec_ref[0, 256:272, :].astype(F32)
        for z in range(1, 8):
            tile = tile + spec_ref[z, 256:272, :].astype(F32)
        tile = split_tile(join_tile(tile)).astype(BF)
        out_ref[:, 16:32, :] = jnp.broadcast_to(tile[None], (32, 16, 128))
    for t in range(16):
        pid = pid_ref[at_ref[0] + 4 * (t // 2) + t % 2]
        acc_ref[:, t, :] = slot_waves(spec_ref, t // 2, t % 2, pid, leg_ref[t])
    if first:
        out_ref[...] = acc_ref[...].astype(BF)
    else:
        out_ref[:, 0:16, :] = acc_ref[...].astype(BF)


def legendre_inverse(pids, at, spec, leg, *extra):
    first = len(extra) > 0
    return pl.pallas_call(
        functools.partial(inverse_kernel, first),
        in_specs=[SMEM, SMEM] + [VMEM] * (2 + len(extra)),
        out_shape=jax.ShapeDtypeStruct((32, 32, 128), BF),
        scratch_shapes=[pltpu.VMEM((32, 32 if first else 16, 128), F32)],
        compiler_params=pltpu.CompilerParams(vmem_limit_bytes=12 << 20),
    )(pids, at, spec, leg, *extra)


def arrange_variance(x_ref, b):
    row, lane = rows((128, 128)), lanes((128, 128))
    keep = jnp.where(row == lane, 1.0, 0.0).astype(BF)
    turn = jnp.where(row + lane == 127, 1.0, 0.0).astype(BF)
    er, el = rows((32, 128)), lanes((32, 128))
    used = (lax.rem(er, 16) < 6) & (lax.rem(el, 32) // 8 == 2 * (er // 16) + lax.rem(er, 2))
    total = None
    for q, (a, order) in enumerate(((b, keep), (7 - b, turn), (8 + b, keep), (15 - b, turn))):
        terms = jnp.concatenate([x_ref[2 * a, 16:32, :], x_ref[2 * a + 1, 16:32, :]], axis=0)
        down = lax.dot_general(order, terms, (((1,), (1,)), ((), ())), preferred_element_type=F32).astype(BF)
        spread = jnp.where(used & (el // 32 == q), 1.0, 0.0).astype(BF)
        part = jnp.dot(down, spread, preferred_element_type=F32)
        total = part if total is None else total + part
    return total


def grid_kernel(first, x_ref, fold_ref, tt_ref, t_ref, *refs):
    x = x_ref[:, 0:16, :].reshape(512, 128)
    if first:
        y_ref, var_ref, hat_ref = refs
        for b in range(4):
            var_ref[128 * b : 128 * b + 128, :] = arrange_variance(x_ref, b)
    else:
        var_ref, y_ref, hat_ref = refs
        tile = jnp.sum(x_ref[:, 16:32, :].astype(F32), axis=0)
        gram = pltpu.roll(join_tile(tile), 120, 1)
        mix = tile_of(splat_factor(gram)[1], True, K)
        mix = jnp.concatenate([mix] * 16, axis=0)
    for g in range(4):
        f = fold_ref[:, 128 * g : 128 * g + 128].astype(F32)
        if first:
            f = jnp.where(lax.rem(rows((128, 128)), 8) == lax.rem(lanes((128, 128)), 8), f, 0.0)
            hat = jnp.dot(x, f.astype(BF), preferred_element_type=F32)
        else:
            f = f * mix
            hi = f.astype(BF)
            low = (f - hi.astype(F32)).astype(BF)
            hat = jnp.dot(x, hi, preferred_element_type=F32) + jnp.dot(x, low, preferred_element_type=F32)
        hat_ref[512 * g : 512 * g + 512, :] = hat.astype(BF)
    grid = jnp.dot(tt_ref[...], hat_ref[...], preferred_element_type=F32)
    scaled = (grid * var_ref[...]).astype(BF)
    lane = lanes((1, 128))
    out = None
    for g in range(4):
        part = jnp.dot(t_ref[512 * g : 512 * g + 512, :], scaled, preferred_element_type=F32)
        sign = jnp.ones((1, 128), F32)
        for q in range(4):
            if SIGNS[g, q] < 0:
                sign = jnp.where((lane >= 32 * q) & (lane < 32 * q + 32), -1.0, sign)
        part = part * sign
        part = part + pltpu.roll(part, 64, 1)
        part = part + pltpu.roll(part, 32, 1)
        out = part if out is None else jnp.where(lane >= 32 * g, part, out)
    y_ref[...] = out.astype(BF).reshape(32, 16, 128)


def grid_stage(x, fold, tt, t, var):
    first = var is None
    y = jax.ShapeDtypeStruct((32, 16, 128), BF)
    return pl.pallas_call(
        functools.partial(grid_kernel, first),
        out_shape=(y, jax.ShapeDtypeStruct((512, 128), F32)) if first else y,
        scratch_shapes=[pltpu.VMEM((2048, 128), BF)],
        compiler_params=pltpu.CompilerParams(vmem_limit_bytes=12 << 20),
    )(*((x, fold, tt, t) if first else (x, fold, tt, t, var)))


def forward_kernel(pid_ref, at_ref, y_ref, leg_ref, out_ref, wide_ref):
    wide_ref[...] = y_ref[...].astype(F32)
    lane = lanes((32, 128))
    for b in range(4):
        zt = jnp.concatenate([wide_ref[:, 4 * b + s, :] for s in range(4)], axis=0).T
        blocks = [
            jnp.concatenate([zt[32 * g + 8 * jj : 32 * g + 8 * jj + 8, :] for g in range(4)], axis=0)
            for jj in range(4)
        ]
        done = []
        for s in range(4):
            t = 4 * b + s
            lhs = None
            for jj in range(4):
                shift = (32 * (jj - s)) % 128
                v = pltpu.roll(blocks[jj], shift, 1) if shift else blocks[jj]
                lhs = v if lhs is None else jnp.where(lane >= 32 * jj, v, lhs)
            p = jnp.dot(lhs.astype(BF), leg_ref[t], preferred_element_type=F32)
            mask = even_mask((16, RP), pid_ref[at_ref[0] + 4 * (t // 2) + t % 2])
            done.append(jnp.where(mask, p[0:16], p[16:32]))
        for u in range(2):
            for n, v in enumerate(pack(done[2 * u : 2 * u + 2], jnp.zeros((16, 128), F32))):
                out_ref[2 * b + u, 16 * n : 16 * n + 16, :] = v


def legendre_forward(pids, at, y, leg):
    return pl.pallas_call(
        forward_kernel,
        in_specs=[SMEM, SMEM, VMEM, VMEM],
        out_shape=jax.ShapeDtypeStruct((8, 272, 128), BF),
        scratch_shapes=[pltpu.VMEM((32, 16, 128), F32)],
        compiler_params=pltpu.CompilerParams(vmem_limit_bytes=12 << 20),
    )(pids, at, y, leg)


def gram_tile(blocks):
    sh = jnp.concatenate(blocks, axis=0)
    hi = sh.astype(BF)
    low = (sh - hi.astype(F32)).astype(BF)
    both = jnp.concatenate([hi, low, jnp.zeros((64, RP), BF)], axis=0)
    full = lax.dot_general(both[0:64], both, (((1,), (1,)), ((), ())), preferred_element_type=F32)
    total = None
    for a in range(2):
        for b in range(2):
            for i in range(4):
                v = full[32 * a + 8 * i : 32 * a + 8 * i + 8, :]
                shift = (128 - (32 * b + 8 * i)) % 128
                v = pltpu.roll(v, shift, 1) if shift else v
                total = v if total is None else total + v
    return jnp.where(lanes((8, 128)) < 8, total, 0.0)


def summed_blocks(parts_ref, table_ref):
    out = []
    for b in range(2):
        total = load_block(parts_ref, 0, b)
        for z in range(1, parts_ref.shape[0]):
            total = total + load_block(parts_ref, z, b)
        out.append(total * table_ref[b : b + 1, :])
    return out


def owner_kernel(parts_ref, table_ref, out_ref):
    sh = summed_blocks(parts_ref, table_ref)
    tile = split_tile(pltpu.roll(gram_tile(sh), 8, 1))
    tile = jnp.concatenate([tile, jnp.zeros((8, 128), F32)], axis=0)
    pieces = pack([sh[b] * table_ref[2 + b : 3 + b, :] for b in range(2)], tile)
    for z in range(out_ref.shape[0]):
        for n, v in enumerate(pieces):
            out_ref[z, 16 * n : 16 * n + 16, :] = v


def owner_step(parts, table):
    return pl.pallas_call(
        owner_kernel,
        out_shape=jax.ShapeDtypeStruct((8, 272, 128), BF),
        compiler_params=pltpu.CompilerParams(vmem_limit_bytes=12 << 20),
    )(parts, table)


def last_kernel(parts_ref, table_ref, sh_ref, gram_ref):
    sh = summed_blocks(parts_ref, table_ref)
    for b in range(2):
        sh_ref[16 * b : 16 * b + 16, :] = sh[b]
    tile = gram_tile(sh)
    line = tile[0:1, :]
    for i in range(1, K):
        line = line + pltpu.roll(tile[i : i + 1, :], 8 * i, 1)
    gram_ref[...] = jnp.broadcast_to(line, gram_ref.shape)


def last_step(parts, table):
    return pl.pallas_call(
        last_kernel,
        out_shape=(jax.ShapeDtypeStruct((32, RP), F32), jax.ShapeDtypeStruct((128, 128), F32)),
        compiler_params=pltpu.CompilerParams(vmem_limit_bytes=12 << 20),
    )(parts, table)


def finish_kernel(sh_ref, gram_ref, other_ref, table_ref, modes_ref, lower_ref):
    line = jnp.sum(gram_ref[...] + other_ref[...], axis=0, keepdims=True)
    row = rows((8, 128))
    gram = jnp.broadcast_to(line, (8, 128))
    for i in range(1, K):
        gram = jnp.where(row == i, jnp.broadcast_to(pltpu.roll(line, 128 - 8 * i, 1), (8, 128)), gram)
    low, inv = splat_factor(gram)
    lower_ref[...] = tile_of(low, False, 0)
    coefs = []
    for q in range(K):
        coef = jnp.zeros((8, 128), F32)
        for i in range(q, K):
            coef = jnp.where(row == i, inv[i][q], coef)
        coefs.append(jnp.concatenate([coef] * (RP // 128), axis=1))
    for b in range(2):
        cos, sin = table_ref[4 + b : 5 + b, :], table_ref[6 + b : 7 + b, :]
        parts = []
        for c in range(2):
            block = sh_ref[16 * b + 8 * c : 16 * b + 8 * c + 8, :]
            out = coefs[0] * block[0:1, :]
            for q in range(1, K):
                out = out + coefs[q] * block[q : q + 1, :]
            parts.append(out)
        for c, v in enumerate((cos * parts[0] + sin * parts[1], sin * parts[0] - cos * parts[1])):
            modes_ref[b, :, c, 0:1024] = v[:, 0:1024]
            modes_ref[b, :, c, 1024:R] = v[:, 1024:R]


def finish(sh, grams, others, table):
    return pl.pallas_call(
        finish_kernel,
        out_shape=(jax.ShapeDtypeStruct((2, K, 2, R), F32), jax.ShapeDtypeStruct((8, 128), F32)),
        compiler_params=pltpu.CompilerParams(vmem_limit_bytes=12 << 20),
    )(sh, grams, others, table)


def body(start_block, legendre, variance, gauss_weight, pair_of_slot):
    lat, zpos, core = lax.axis_index("lat"), lax.axis_index("z"), lax.axis_index("c")
    at = jnp.stack([lat * 32 + core * 2, zpos * 4, core]).astype(jnp.int32)
    got = lax.ppermute(legendre, "c", [(0, 1), (1, 0)])
    spec, table = start_step(pair_of_slot, at, start_block)
    spec = lax.all_to_all(spec, "z", 0, 0, tiled=True)

    both = combine(at, legendre, got)
    pids = pair_of_slot.reshape(16, 8, 2, 2).transpose(0, 2, 1, 3).reshape(1, 512)
    place = jnp.where(pids % 2 == 0, pids, T_SIZE - pids) // 2
    t, tt = slot_tables(place)
    spec, both, t, tt = lax.optimization_barrier((spec, both, t, tt))
    fold = jnp.asarray(fold_matrix(), BF)

    for step in range(STEPS):
        if step == 0:
            x = legendre_inverse(pair_of_slot, at, spec, both, variance, gauss_weight.reshape(1, 64))
        else:
            spec = lax.all_to_all(spec, "z", 0, 0, tiled=True)
            x = legendre_inverse(pair_of_slot, at, spec, both)
        x = lax.all_to_all(x, ("lat", "c"), 0, 0, tiled=True)
        if step == 0:
            y, var = grid_stage(x, fold, tt, t, None)
        else:
            y = grid_stage(x, fold, tt, t, var)
        y = lax.all_to_all(y, ("lat", "c"), 0, 0, tiled=True)
        parts = legendre_forward(pair_of_slot, at, y, both)
        parts = lax.all_to_all(parts, "z", 0, 0, tiled=True)
        if step + 1 < STEPS:
            spec = owner_step(parts, table)
    sh, gram = last_step(parts, table)
    grams = lax.all_to_all(gram.reshape(128, 1, 128), ("lat", "z"), 0, 0, tiled=True).reshape(128, 128)
    others = lax.ppermute(grams, "c", [(0, 1), (1, 0)])
    modes, lower = finish(sh, grams, others, table)
    return modes, lower[:, :K]


def solution(mesh):
    fine = Mesh(mesh.devices.reshape(16, 8, 2), ("lat", "z", "c"))
    placed = (
        P(("lat", "z", "c"), None, None, None),
        P("lat", ("z", "c"), None),
        P(("z", "c"), "lat"),
        P(("z", "c")),
        P(),
    )
    return jax.shard_map(
        body,
        mesh=fine,
        in_specs=placed,
        out_specs=(P(("lat", "z", "c"), None, None, None), P()),
        check_vma=False,
    )
```

time: 937 us -> 260 us (0.28)
  waiting for transfers between devices: 594 us -> 1.93 us
  matrix products: 52.2 us -> 0 us
  blocking collectives: 239 us -> 198 us
  Pallas kernels: 0 us -> 32.6 us
  other arithmetic: 20.5 us -> 0.1 us
  between operations: 14.5 us -> 0.78 us
  starting transfers between devices: 1.16 us -> 11.8 us
    all_gather x9 -> x0, waiting for transfers between devices: 428 us -> none  [the longest x3 162 us: body(): lax.all_gather(waves, 'lat', axis=0, tiled=True)]
    psum x3 -> x0, blocking collectives: 239 us -> none  [body(): gram = lax.psum(gram_of(shaped), ('lat', 'lon'))]
    all_to_all x0 -> x12, blocking collectives: none -> 198 us  [the longest x3 64.5 us: body(): parts = lax.all_to_all(parts, 'z', 0, 0, tiled=True)]
    reduce_scatter x3 -> x0, waiting for transfers between devices: 166 us -> none  [body(): lax.psum_scatter(degree_terms(spectral_grid, legendre, first).astype(jnp....]
    dot_general x18 -> x0, matrix products: 51.6 us -> none  [the longest x3 15.3 us: body(): jnp.einsum('shkcj,shcl->kjl', lax.all_gather(waves, 'lat', axis=0, tiled=...]
    pallas_call x0 -> x16, Pallas kernels: none -> 32.6 us  [the longest x3 9.33 us: grid_stage(): pl.pallas_call(functools.partial(grid_kernel, first), out_shape=(y, jax.S...]
    another operation x24 -> x1, other arithmetic: 15.4 us -> 0.08 us  [body(): at = jnp.stack([lat * 32 + core * 2, zpos * 4, core]).astype(jnp.int32)]
  transfers between devices with their start and end apart: 12 -> 3, of which waited for: 12 -> 2; matrix products, arithmetic and copies ran while one was open for 1% -> 0% of each run, Pallas kernels for 0% -> 4%
where the time goes in v2:
time: 260 us; the launch traced here: 259 us
  blocking collectives  198 us (76%)
  Pallas kernels  32.6 us (13%)
  local copies, waits for them, and re-layouts  14 us (5%)
  starting transfers between devices  11.8 us (5%)
    all_to_all x3, blocking collectives, body(): parts = lax.all_to_all(parts, 'z', 0, 0, tiled=True)  64.5 us
    all_to_all x3, blocking collectives, body(): x = lax.all_to_all(x, ('lat', 'c'), 0, 0, tiled=True)  45.9 us
    all_to_all x2, blocking collectives, body(): spec = lax.all_to_all(spec, 'z', 0, 0, tiled=True)  37.5 us
    all_to_all x3, blocking collectives, body(): y = lax.all_to_all(y, ('lat', 'c'), 0, 0, tiled=True)  33.5 us
    all_to_all x1, blocking collectives, body(): lax.all_to_all(gram.reshape(128, 1, 128), ('lat', 'z'), 0, 0, tiled=True)  16.1 us
    unnamed x28, local copies, waits for them, and re-layouts  12.9 us
    pallas_call x3, Pallas kernels, grid_stage(): pl.pallas_call(functools.partial(grid_kernel, first), out_shape=(y, jax.S...  9.33 us
    pallas_call x3, Pallas kernels, legendre_inverse(): pl.pallas_call(functools.partial(inverse_kernel, first), in_specs=[SMEM,...  6.71 us
  transfers between devices with their start and end apart: 3, of which 2 were waited for; matrix products, arithmetic and copies ran while one was open for 0% of the time, Pallas kernels for 4%

profile of v2, /device:TPU:1, one launch (start us, length us, event | category | flops | bytes accessed | tf_op | source)
XLA Modules:
  0.0 258.8 jit_solution(10084397034664396094)
XLA Ops:
  0.6 3.3 %collective-permute-start = (bf16[32,64,1025]{2,1,0:T(8,128)(2,1)}, bf16[32,64,1025]{2,1,0:T(8,128)(2,1)}, u32[]{:S(2)}, u32[]{:S(2)}) collective-permute-start(bf16[32,64,1025]{2,1,0:T(8,128)(2,1)} %leg_ref.1), channel_id=1, source_target_pairs={{0,1},{1,0},{2,3},{3,2},{4,5},{5,4},{6,7},{7,6},{8,9},{9,8},{10,11... | collective-permute-start | bytes 12595208 | tf_op jit(solution)/shard_map/ppermute | solution.py:470
  4.0 0.1 pad_add_fusion.at_ref
  4.0 0.0 copy-start.9
  4.0 0.9 copy-done.9
  4.9 0.0 copy-start.10
  4.9 0.7 copy-done.10
  5.6 1.7 shard_map.95
  7.3 6.5 %all-to-all-start = ((bf16[8,272,128]{2,1,0:T(8,128)(2,1)}), bf16[8,272,128]{2,1,0:T(8,128)(2,1)S(1)}, u32[]{:S(2)}, u32[]{:S(2)}) async-start(bf16[8,272,128]{2,1,0:T(8,128)(2,1)} %get-tuple-element.16), calls=%async_computation | async-start | bytes 1114112 | tf_op jit(solution)/shard_map/all_to_all | solution.py:472
  13.7 0.9 reshape.169
  14.7 0.1 reshape.170
  14.8 0.0 copy-start.6
  14.8 1.6 copy-done.6
  16.4 0.0 copy-start.7
  16.4 1.6 copy-done.7
  18.0 2.4 shard_map.97
  20.5 0.0 copy-start.3
  20.5 1.3 copy-done.3
  21.8 0.0 collective-permute-done.got_ref
  21.8 0.0 copy-start.5
  21.8 2.3 copy-done.5
  24.2 0.0 copy-start.11
  24.2 0.0 copy-start.12
  24.2 0.0 copy-start.13
  24.2 5.1 %shard_map.96.leg_ref = bf16[16,128,1152]{2,1,0:T(8,128)(2,1)S(1)} custom-call(s32[3]{0:T(128)S(1)} %pad_add_fusion.at_ref, bf16[32,64,1025]{2,1,0:T(8,128)(2,1)S(1)} %copy-done.5, bf16[32,64,1025]{2,1,0:T(8,128)(2,1)} %collective-permute-done.got_ref), custom_call_target="tpu_custom_call" | custom-call | tf_op jit(solution)/shard_map/pallas_call | solution.py:213
  29.3 0.0 copy-start
  29.3 2.1 copy-done
  31.4 1.0 all-to-all-done.spec_ref
  32.5 0.0 copy-done.11
  32.5 0.0 copy-done.12
  32.5 0.0 copy-done.13
  32.5 0.0 copy-start.1
  32.5 2.3 copy-done.1
  34.8 0.0 copy-start.4
  34.8 0.0 copy-start.8
  34.8 2.3 shard_map.98
  37.2 16.4 %all_to_all.65.x_ref = bf16[32,32,128]{2,1,0:T(8,128)(2,1)S(1)} all-to-all(bf16[32,32,128]{2,1,0:T(8,128)(2,1)S(1)} %shard_map.98), channel_id=1, replica_groups=mesh['lat'=16,'z'=8,'c'=2] {'lat','c'}, dimensions={0} | all-to-all | bytes 524288 | tf_op jit(solution)/shard_map/all_to_all | solution.py:487
  53.5 0.0 copy-done.4
  53.5 0.0 copy-done.8
  53.5 3.0 %shard_map.99 = (bf16[32,16,128]{2,1,0:T(8,128)(2,1)S(1)}, f32[512,128]{1,0:T(8,128)S(1)}) custom-call(bf16[32,32,128]{2,1,0:T(8,128)(2,1)S(1)} %all_to_all.65.x_ref, bf16[128,512]{1,0:T(8,128)(2,1)S(1)} %copy-done.8, bf16[512,2048]{1,0:T(8,128)(2,1)S(1)} %copy-done.4, bf16[2048,512]{1,0:T(8,128)(2,1)S(1)} %get-tuple-element.22.t_ref), custom_call_target="tpu_custom_call" | custom-call | tf_op jit(solution)/shard_map/pallas_call | solution.py:324
  56.5 11.2 %all_to_all.66.y_ref = bf16[32,16,128]{2,1,0:T(8,128)(2,1)S(1)} all-to-all(bf16[32,16,128]{2,1,0:T(8,128)(2,1)S(1)} %get-tuple-element.23), channel_id=1, replica_groups=mesh['lat'=16,'z'=8,'c'=2] {'lat','c'}, dimensions={0} | all-to-all | bytes 262144 | tf_op jit(solution)/shard_map/all_to_all | solution.py:492
  67.7 0.0 copy-done.2
  67.7 1.6 shard_map.100
  69.3 23.2 %all_to_all.67.parts_ref = bf16[8,272,128]{2,1,0:T(8,128)(2,1)S(1)} all-to-all(bf16[8,272,128]{2,1,0:T(8,128)(2,1)S(1)} %shard_map.100), channel_id=1, replica_groups=mesh['lat'=16,'z'=8,'c'=2] {'z'}, dimensions={0} | all-to-all | bytes 1114112 | tf_op jit(solution)/shard_map/all_to_all | solution.py:494
  92.5 0.5 shard_map.101
  93.0 18.5 %all_to_all.68.spec_ref = bf16[8,272,128]{2,1,0:T(8,128)(2,1)S(1)} all-to-all(bf16[8,272,128]{2,1,0:T(8,128)(2,1)S(1)} %shard_map.101), channel_id=1, replica_groups=mesh['lat'=16,'z'=8,'c'=2] {'z'}, dimensions={0} | all-to-all | bytes 1114112 | tf_op jit(solution)/shard_map/all_to_all | solution.py:485
  111.5 2.2 shard_map.102
  113.7 15.1 %all_to_all.69.x_ref = bf16[32,32,128]{2,1,0:T(8,128)(2,1)S(1)} all-to-all(bf16[32,32,128]{2,1,0:T(8,128)(2,1)S(1)} %shard_map.102), channel_id=1, replica_groups=mesh['lat'=16,'z'=8,'c'=2] {'lat','c'}, dimensions={0} | all-to-all | bytes 524288 | tf_op jit(solution)/shard_map/all_to_all | solution.py:487
  128.8 3.2 %shard_map.103 = bf16[32,16,128]{2,1,0:T(8,128)(2,1)S(1)} custom-call(bf16[32,32,128]{2,1,0:T(8,128)(2,1)S(1)} %all_to_all.69.x_ref, bf16[128,512]{1,0:T(8,128)(2,1)S(1)} %copy-done.8, bf16[512,2048]{1,0:T(8,128)(2,1)S(1)} %copy-done.4, bf16[2048,512]{1,0:T(8,128)(2,1)S(1)} %get-tuple-element.22.t_ref, f32[512,128]{1,0:T(8,128)S(1)} %get-tuple-element.25.refs_0_), custom_call_target="tpu_custom_call" | custom-call | tf_op jit(solution)/shard_map/pallas_call | solution.py:324
  131.9 11.2 %all_to_all.70.y_ref = bf16[32,16,128]{2,1,0:T(8,128)(2,1)S(1)} all-to-all(bf16[32,16,128]{2,1,0:T(8,128)(2,1)S(1)} %shard_map.103), channel_id=1, replica_groups=mesh['lat'=16,'z'=8,'c'=2] {'lat','c'}, dimensions={0} | all-to-all | bytes 262144 | tf_op jit(solution)/shard_map/all_to_all | solution.py:492
  143.1 1.6 shard_map.104
  144.8 20.6 %all_to_all.71.parts_ref = bf16[8,272,128]{2,1,0:T(8,128)(2,1)S(1)} all-to-all(bf16[8,272,128]{2,1,0:T(8,128)(2,1)S(1)} %shard_map.104), channel_id=1, replica_groups=mesh['lat'=16,'z'=8,'c'=2] {'z'}, dimensions={0} | all-to-all | bytes 1114112 | tf_op jit(solution)/shard_map/all_to_all | solution.py:494
  165.4 0.5 shard_map.105
  165.9 19.1 %all_to_all.72.spec_ref = bf16[8,272,128]{2,1,0:T(8,128)(2,1)S(1)} all-to-all(bf16[8,272,128]{2,1,0:T(8,128)(2,1)S(1)} %shard_map.105), channel_id=1, replica_groups=mesh['lat'=16,'z'=8,'c'=2] {'z'}, dimensions={0} | all-to-all | bytes 1114112 | tf_op jit(solution)/shard_map/all_to_all | solution.py:485
  185.0 2.2 shard_map.106
  187.2 14.5 %all_to_all.73.x_ref = bf16[32,32,128]{2,1,0:T(8,128)(2,1)S(1)} all-to-all(bf16[32,32,128]{2,1,0:T(8,128)(2,1)S(1)} %shard_map.106), channel_id=1, replica_groups=mesh['lat'=16,'z'=8,'c'=2] {'lat','c'}, dimensions={0} | all-to-all | bytes 524288 | tf_op jit(solution)/shard_map/all_to_all | solution.py:487
  201.6 3.2 %shard_map.107 = bf16[32,16,128]{2,1,0:T(8,128)(2,1)S(1)} custom-call(bf16[32,32,128]{2,1,0:T(8,128)(2,1)S(1)} %all_to_all.73.x_ref, bf16[128,512]{1,0:T(8,128)(2,1)S(1)} %copy-done.8, bf16[512,2048]{1,0:T(8,128)(2,1)S(1)} %copy-done.4, bf16[2048,512]{1,0:T(8,128)(2,1)S(1)} %get-tuple-element.22.t_ref, f32[512,128]{1,0:T(8,128)S(1)} %get-tuple-element.25.refs_0_), custom_call_target="tpu_custom_call" | custom-call | tf_op jit(solution)/shard_map/pallas_call | solution.py:324
  204.8 11.2 %all_to_all.74.y_ref = bf16[32,16,128]{2,1,0:T(8,128)(2,1)S(1)} all-to-all(bf16[32,16,128]{2,1,0:T(8,128)(2,1)S(1)} %shard_map.107), channel_id=1, replica_groups=mesh['lat'=16,'z'=8,'c'=2] {'lat','c'}, dimensions={0} | all-to-all | bytes 262144 | tf_op jit(solution)/shard_map/all_to_all | solution.py:492
  216.0 1.6 shard_map.108
  217.6 20.6 %all_to_all.75.parts_ref = bf16[8,272,128]{2,1,0:T(8,128)(2,1)S(1)} all-to-all(bf16[8,272,128]{2,1,0:T(8,128)(2,1)S(1)} %shard_map.108), channel_id=1, replica_groups=mesh['lat'=16,'z'=8,'c'=2] {'z'}, dimensions={0} | all-to-all | bytes 1114112 | tf_op jit(solution)/shard_map/all_to_all | solution.py:494
  238.3 0.4 shard_map.109
  238.7 16.1 %all_to_all.76 = f32[128,1,128]{2,1,0:T(1,128)S(1)} all-to-all(f32[128,1,128]{2,1,0:T(1,128)S(1)} %bitcast.14), channel_id=1, replica_groups=mesh['lat'=16,'z'=8,'c'=2] {'lat','z'}, dimensions={0} | all-to-all | bytes 131072 | tf_op jit(solution)/shard_map/all_to_all | solution.py:498
  254.8 2.0 collective-permute-start.1
  256.8 0.9 collective-permute-done.1.other_ref
  257.7 1.1 shard_map.110
  (3 shorter events, 0.0 us)
Async XLA Ops:
  0.6 21.2 %collective-permute-start = (bf16[32,64,1025]{2,1,0:T(8,128)(2,1)}, bf16[32,64,1025]{2,1,0:T(8,128)(2,1)}, u32[]{:S(2)}, u32[]{:S(2)}) collective-permute-start(bf16[32,64,1025]{2,1,0:T(8,128)(2,1)} %leg_ref.1), channel_id=1, source_target_pairs={{0,1},{1,0},{2,3},{3,2},{4,5},{5,4},{6,7},{7,6},{8,9},{9,8},{10,11... | collective-permute-start | bytes 12595208 | tf_op jit(solution)/shard_map/ppermute | solution.py:470
  4.0 0.9 copy-start.9
  4.9 0.7 copy-start.10
  7.3 25.2 %all-to-all-start = ((bf16[8,272,128]{2,1,0:T(8,128)(2,1)}), bf16[8,272,128]{2,1,0:T(8,128)(2,1)S(1)}, u32[]{:S(2)}, u32[]{:S(2)}) async-start(bf16[8,272,128]{2,1,0:T(8,128)(2,1)} %get-tuple-element.16), calls=%async_computation | async-start | bytes 1114112 | tf_op jit(solution)/shard_map/all_to_all | solution.py:472
  14.8 1.6 copy-start.6
  16.4 1.6 copy-start.7
  20.5 1.4 copy-start.3
  21.8 2.3 copy-start.5
  24.2 8.3 %copy-start.11 = (s32[512]{0:T(512)S(1)}, s32[512]{0:T(512)}, u32[]{:S(2)}) copy-start(s32[512]{0:T(512)} %pid_ref.13) | copy-start | bytes 6148
  24.2 8.3 %copy-start.12 = (f32[64,128]{1,0:T(8,128)S(1)}, f32[64,128]{1,0:T(8,128)}, u32[]{:S(2)}) copy-start(f32[64,128]{1,0:T(8,128)} %refs_0_.1) | copy-start | bytes 98308
  24.2 8.3 %copy-start.13 = (f32[64]{0:T(128)S(1)}, f32[64]{0:T(128)}, u32[]{:S(2)}) copy-start(f32[64]{0:T(128)} %param.11) | copy-start | bytes 772
  29.3 2.1 copy-start
  32.5 2.3 copy-start.1
  34.8 18.7 %copy-start.4 = (bf16[512,2048]{1,0:T(8,128)(2,1)S(1)}, bf16[512,2048]{1,0:T(8,128)(2,1)}, u32[]{:S(2)}) copy-start(bf16[512,2048]{1,0:T(8,128)(2,1)} %copy-done.3) | copy-start | bytes 6291460
  34.8 18.7 %copy-start.8 = (bf16[128,512]{1,0:T(8,128)(2,1)S(1)}, bf16[128,512]{1,0:T(8,128)(2,1)}, u32[]{:S(2)}) copy-start(bf16[128,512]{1,0:T(8,128)(2,1)} %constant.54.clone.fold_ref) | copy-start | bytes 393220
  53.5 14.1 %copy-start.2 = (bf16[16,128,1152]{2,1,0:T(8,128)(2,1)S(1)}, bf16[16,128,1152]{2,1,0:T(8,128)(2,1)}, u32[]{:S(2)}) copy-start(bf16[16,128,1152]{2,1,0:T(8,128)(2,1)} %copy-done) | copy-start | bytes 14155780
  254.8 2.9 %collective-permute-start.1 = (f32[128,128]{1,0:T(8,128)S(1)}, f32[128,128]{1,0:T(8,128)S(1)}, u32[]{:S(2)}, u32[]{:S(2)}) collective-permute-start(f32[128,128]{1,0:T(8,128)S(1)} %bitcast.12), channel_id=1, source_target_pairs={{0,1},{1,0},{2,3},{3,2},{4,5},{5,4},{6,7},{7,6},{8,9},{9,8},{10,11... | collective-permute-start | bytes 196616 | tf_op jit(solution)/shard_map/ppermute | solution.py:499

commit v3 on v2

--- a/solution.py
+++ b/solution.py
@@ -25,7 +25,7 @@
 
 def natural_tables():
     q = np.arange(512)[:, None]
-    i2 = 2 * np.arange(512)[None, :] + 1
+    i2 = 2 * np.arange(256)[None, :] + 1
     out = []
     for m in (2 * q, 1023 - 2 * q):
         angle = (m * i2 % 4096) * (2.0 * math.pi / 4096)
@@ -109,17 +109,24 @@
 
 def load_block(ref, z, b):
     main = [ref[z, (b * 8 + l) * 16 : (b * 8 + l) * 16 + 16, :].astype(F32) for l in range(8)]
-    extra = ref[z, 256:272, :].astype(F32)
-    if b:
-        extra = pltpu.roll(extra, 128 - b, 1)
-    return jnp.concatenate(main + [jnp.where(lanes((16, 128)) == 0, extra, 0.0)], axis=1)
+    extra = ref[z, 256:264, :].astype(F32)
+    last = [pltpu.roll(extra, 128 - n, 1) if n else extra for n in (2 * b, 2 * b + 1)]
+    last = jnp.concatenate(last, axis=0)
+    return jnp.concatenate(main + [jnp.where(lanes((16, 128)) == 0, last, 0.0)], axis=1)
 
 
 def pack(blocks, tile):
-    lane = lanes((16, 128))
+    lane = lanes((8, 128))
     pieces = [v[:, 128 * l : 128 * l + 128].astype(BF) for v in blocks for l in range(8)]
-    extra = jnp.where(lane == 0, blocks[0][:, 1024:RP], jnp.where(lane == 1, pltpu.roll(blocks[1][:, 1024:RP], 1, 1), tile))
-    return pieces + [extra.astype(BF)]
+    for n in range(4):
+        col = blocks[n // 2][8 * (n % 2) : 8 * (n % 2) + 8, 1024:RP]
+        tile = jnp.where(lane == n, pltpu.roll(col, n, 1) if n else col, tile)
+    return pieces + [tile.astype(BF)]
+
+
+def put(out_ref, z, pieces):
+    for n, v in enumerate(pieces):
+        out_ref[z, 16 * n : 16 * n + v.shape[0], :] = v
 
 
 def start_kernel(pid_ref, at_ref, start_ref, out_ref, table_ref):
@@ -149,42 +156,48 @@
         re, im = half
         cb, sb, wb = cos[b : b + 1], sin[b : b + 1], weight[b : b + 1]
         blocks.append(jnp.concatenate([wb * (re * cb + im * sb), wb * (re * sb - im * cb)], axis=0))
-    pieces = pack(blocks, jnp.zeros((16, 128), F32))
+    pieces = pack(blocks, jnp.zeros((8, 128), F32))
     for z in range(out_ref.shape[0]):
-        for n, v in enumerate(pieces):
-            out_ref[z, 16 * n : 16 * n + 16, :] = v
+        put(out_ref, z, pieces)
 
 
 SMEM = pl.BlockSpec(memory_space=pltpu.SMEM)
 VMEM = pl.BlockSpec(memory_space=pltpu.VMEM)
+HBM = pl.BlockSpec(memory_space=pltpu.HBM)
 
 
 def start_step(pids, at, start):
     return pl.pallas_call(
         start_kernel,
         in_specs=[SMEM, SMEM, VMEM],
-        out_shape=(jax.ShapeDtypeStruct((8, 272, 128), BF), jax.ShapeDtypeStruct((8, RP), F32)),
+        out_shape=(jax.ShapeDtypeStruct((8, 264, 128), BF), jax.ShapeDtypeStruct((8, RP), F32)),
         compiler_params=pltpu.CompilerParams(vmem_limit_bytes=12 << 20),
     )(pids, at, start)
 
 
-def table_kernel(place_ref, nat_ref, natt_ref, t_ref, tt_ref):
+def table_kernel(place_ref, nat_ref, natt_ref, t_ref, tt_ref, sign_ref):
     hot = jnp.where(rows((512, 512)) == place_ref[...], 1.0, 0.0)
     hot_s = hot.T.astype(BF)
     hot = hot.astype(BF)
     for g in range(4):
         t_ref[512 * g : 512 * g + 512, :] = jnp.dot(hot_s, nat_ref[512 * g : 512 * g + 512, :], preferred_element_type=F32).astype(BF)
         tt_ref[:, 512 * g : 512 * g + 512] = jnp.dot(natt_ref[:, 512 * g : 512 * g + 512], hot, preferred_element_type=F32).astype(BF)
+    turn = jnp.where(lax.rem(rows((512, 128)), 2) == 0, 1.0, -1.0).astype(BF)
+    sign_ref[...] = jnp.dot(hot_s, turn, preferred_element_type=F32)
 
 
 def slot_tables(place):
     nat = natural_tables()
-    natt = np.ascontiguousarray(nat.transpose(2, 0, 1)).reshape(512, 2048)
+    natt = np.ascontiguousarray(nat.transpose(2, 0, 1)).reshape(256, 2048)
     return pl.pallas_call(
         table_kernel,
-        out_shape=(jax.ShapeDtypeStruct((2048, 512), BF), jax.ShapeDtypeStruct((512, 2048), BF)),
-        compiler_params=pltpu.CompilerParams(vmem_limit_bytes=12 << 20),
-    )(place, jnp.asarray(nat.reshape(2048, 512)), jnp.asarray(natt))
+        out_shape=(
+            jax.ShapeDtypeStruct((2048, 256), BF),
+            jax.ShapeDtypeStruct((256, 2048), BF),
+            jax.ShapeDtypeStruct((512, 128), F32),
+        ),
+        compiler_params=pltpu.CompilerParams(vmem_limit_bytes=12 << 20),
+    )(place, jnp.asarray(nat.reshape(2048, 256)), jnp.asarray(natt))
 
 
 def slot_waves(spec_ref, z, b, pid, leg):
@@ -198,35 +211,43 @@
     return jnp.where(lane < 32, p[0:32], jnp.where(lane < 64, p[32:64], jnp.where(lane < 96, p[64:96], p[96:128])))
 
 
-def combine_kernel(at_ref, leg_ref, got_ref, both_ref):
+def combine_kernel(at_ref, leg_ref, got_ref, both_ref, sems):
     core = at_ref[2]
-    lane = lanes((64, 128))
-    for b in range(2):
-        for ref, half in ((leg_ref, core), (got_ref, 1 - core)):
-            at = pl.ds(pl.multiple_of(half * 64, 64), 64)
-            both_ref[b, at, 0:1024] = ref[b, :, 0:1024]
-            col = jnp.broadcast_to(ref[b, :, 1024:R].astype(F32), (64, 128))
-            both_ref[b, at, 1024:RP] = jnp.where(lane == 0, col, 0.0).astype(BF)
+    copies = []
+    for z in range(8):
+        for n, (ref, half) in enumerate(((leg_ref, core), (got_ref, 1 - core))):
+            copy = pltpu.make_async_copy(
+                ref.at[pl.ds(4 * z + 2 * core, 2)],
+                both_ref.at[pl.ds(2 * z, 2), pl.ds(pl.multiple_of(half * 64, 64), 64)],
+                sems.at[2 * z + n],
+            )
+            copy.start()
+            copies.append(copy)
+    for copy in copies:
+        copy.wait()
 
 
 def combine(at, leg, got):
     return pl.pallas_call(
         combine_kernel,
-        grid_spec=pltpu.PrefetchScalarGridSpec(
-            num_scalar_prefetch=1,
-            grid=(8,),
-            in_specs=[pl.BlockSpec((2, 64, R), lambda i, at: (2 * i + at[2], 0, 0))] * 2,
-            out_specs=pl.BlockSpec((2, 128, RP), lambda i, at: (i, 0, 0)),
-        ),
-        out_shape=jax.ShapeDtypeStruct((16, 128, RP), BF),
+        in_specs=[SMEM, HBM, HBM],
+        out_specs=HBM,
+        out_shape=jax.ShapeDtypeStruct((16, 128, R), BF),
+        scratch_shapes=[pltpu.SemaphoreType.DMA((16,))],
         compiler_params=pltpu.CompilerParams(vmem_limit_bytes=8 << 20),
     )(at, leg, got)
+
+
+def whole(leg_ref, t):
+    last = jnp.broadcast_to(leg_ref[t, :, 1024:R].astype(F32), (128, 128))
+    last = jnp.where(lanes((128, 128)) == 0, last, 0.0).astype(BF)
+    return jnp.concatenate([leg_ref[t, :, 0:1024], last], axis=1)
 
 
 def inverse_kernel(first, pid_ref, at_ref, spec_ref, leg_ref, *refs):
     if first:
         var_ref, gauss_ref, out_ref, acc_ref = refs
-        acc_ref[:, 16:32, :] = jnp.zeros((32, 16, 128), F32)
+        acc_ref[:, 16:24, :] = jnp.zeros((32, 8, 128), F32)
         gauss = jnp.broadcast_to(gauss_ref[...], (64, 64))
         gauss = jnp.sum(jnp.where(rows((64, 64)) == lanes((64, 64)), gauss, 0.0), axis=1, keepdims=True)
         rest = var_ref[...] * gauss
@@ -237,14 +258,14 @@
                 acc_ref[:, 16 + 2 * n + jh, :] = term[32 * jh : 32 * jh + 32, :]
     else:
         out_ref, acc_ref = refs
-        tile = spec_ref[0, 256:272, :].astype(F32)
+        tile = spec_ref[0, 256:264, :].astype(F32)
         for z in range(1, 8):
-            tile = tile + spec_ref[z, 256:272, :].astype(F32)
+            tile = tile + spec_ref[z, 256:264, :].astype(F32)
         tile = split_tile(join_tile(tile)).astype(BF)
-        out_ref[:, 16:32, :] = jnp.broadcast_to(tile[None], (32, 16, 128))
+        out_ref[:, 16:24, :] = jnp.broadcast_to(tile[None], (32, 8, 128))
     for t in range(16):
         pid = pid_ref[at_ref[0] + 4 * (t // 2) + t % 2]
-        acc_ref[:, t, :] = slot_waves(spec_ref, t // 2, t % 2, pid, leg_ref[t])
+        acc_ref[:, t, :] = slot_waves(spec_ref, t // 2, t % 2, pid, whole(leg_ref, t))
     if first:
         out_ref[...] = acc_ref[...].astype(BF)
     else:
@@ -256,8 +277,8 @@
     return pl.pallas_call(
         functools.partial(inverse_kernel, first),
         in_specs=[SMEM, SMEM] + [VMEM] * (2 + len(extra)),
-        out_shape=jax.ShapeDtypeStruct((32, 32, 128), BF),
-        scratch_shapes=[pltpu.VMEM((32, 32 if first else 16, 128), F32)],
+        out_shape=jax.ShapeDtypeStruct((32, 24, 128), BF),
+        scratch_shapes=[pltpu.VMEM((32, 24 if first else 16, 128), F32)],
         compiler_params=pltpu.CompilerParams(vmem_limit_bytes=12 << 20),
     )(pids, at, spec, leg, *extra)
 
@@ -266,30 +287,37 @@
     row, lane = rows((128, 128)), lanes((128, 128))
     keep = jnp.where(row == lane, 1.0, 0.0).astype(BF)
     turn = jnp.where(row + lane == 127, 1.0, 0.0).astype(BF)
-    er, el = rows((32, 128)), lanes((32, 128))
-    used = (lax.rem(er, 16) < 6) & (lax.rem(el, 32) // 8 == 2 * (er // 16) + lax.rem(er, 2))
-    total = None
-    for q, (a, order) in enumerate(((b, keep), (7 - b, turn), (8 + b, keep), (15 - b, turn))):
-        terms = jnp.concatenate([x_ref[2 * a, 16:32, :], x_ref[2 * a + 1, 16:32, :]], axis=0)
-        down = lax.dot_general(order, terms, (((1,), (1,)), ((), ())), preferred_element_type=F32).astype(BF)
-        spread = jnp.where(used & (el // 32 == q), 1.0, 0.0).astype(BF)
-        part = jnp.dot(down, spread, preferred_element_type=F32)
-        total = part if total is None else total + part
-    return total
-
-
-def grid_kernel(first, x_ref, fold_ref, tt_ref, t_ref, *refs):
+    er, el = rows((16, 128)), lanes((16, 128))
+    used = (lax.rem(er, 8) < 6) & (lax.rem(el, 32) // 8 == 2 * (er // 8) + lax.rem(er, 2))
+    halves = []
+    for places in (
+        ((b, keep), (7 - b, turn), (8 + b, keep), (15 - b, turn)),
+        ((3 - b, turn), (4 + b, keep), (11 - b, turn), (12 + b, keep)),
+    ):
+        total = None
+        for q, (a, order) in enumerate(places):
+            terms = jnp.concatenate([x_ref[2 * a, 16:24, :], x_ref[2 * a + 1, 16:24, :]], axis=0)
+            down = lax.dot_general(order, terms, (((1,), (1,)), ((), ())), preferred_element_type=F32).astype(BF)
+            spread = jnp.where(used & (el // 32 == q), 1.0, 0.0).astype(BF)
+            part = jnp.dot(down, spread, preferred_element_type=F32)
+            total = part if total is None else total + part
+        halves.append(total)
+    return jnp.concatenate(halves, axis=1)
+
+
+def grid_kernel(first, x_ref, fold_ref, tt_ref, t_ref, sign_ref, *refs):
     x = x_ref[:, 0:16, :].reshape(512, 128)
     if first:
         y_ref, var_ref, hat_ref = refs
-        for b in range(4):
+        for b in range(2):
             var_ref[128 * b : 128 * b + 128, :] = arrange_variance(x_ref, b)
     else:
         var_ref, y_ref, hat_ref = refs
-        tile = jnp.sum(x_ref[:, 16:32, :].astype(F32), axis=0)
+        tile = jnp.sum(x_ref[:, 16:24, :].astype(F32), axis=0)
         gram = pltpu.roll(join_tile(tile), 120, 1)
         mix = tile_of(splat_factor(gram)[1], True, K)
         mix = jnp.concatenate([mix] * 16, axis=0)
+    sign = sign_ref[...]
     for g in range(4):
         f = fold_ref[:, 128 * g : 128 * g + 128].astype(F32)
         if first:
@@ -300,33 +328,38 @@
             hi = f.astype(BF)
             low = (f - hi.astype(F32)).astype(BF)
             hat = jnp.dot(x, hi, preferred_element_type=F32) + jnp.dot(x, low, preferred_element_type=F32)
-        hat_ref[512 * g : 512 * g + 512, :] = hat.astype(BF)
+        turned = hat * sign if g == 0 else hat * -sign
+        to = (0, 1, 3, 2)[g]
+        hat_ref[512 * g : 512 * g + 512, 0:128] = hat.astype(BF)
+        hat_ref[512 * to : 512 * to + 512, 128:256] = turned.astype(BF)
     grid = jnp.dot(tt_ref[...], hat_ref[...], preferred_element_type=F32)
     scaled = (grid * var_ref[...]).astype(BF)
     lane = lanes((1, 128))
+    parts = [jnp.dot(t_ref[512 * g : 512 * g + 512, :], scaled, preferred_element_type=F32) for g in range(4)]
     out = None
     for g in range(4):
-        part = jnp.dot(t_ref[512 * g : 512 * g + 512, :], scaled, preferred_element_type=F32)
-        sign = jnp.ones((1, 128), F32)
+        turned = parts[(0, 1, 3, 2)[g]][:, 128:256]
+        part = parts[g][:, 0:128] + (turned * sign if g == 0 else turned * -sign)
+        flip = jnp.ones((1, 128), F32)
         for q in range(4):
             if SIGNS[g, q] < 0:
-                sign = jnp.where((lane >= 32 * q) & (lane < 32 * q + 32), -1.0, sign)
-        part = part * sign
+                flip = jnp.where((lane >= 32 * q) & (lane < 32 * q + 32), -1.0, flip)
+        part = part * flip
         part = part + pltpu.roll(part, 64, 1)
         part = part + pltpu.roll(part, 32, 1)
         out = part if out is None else jnp.where(lane >= 32 * g, part, out)
     y_ref[...] = out.astype(BF).reshape(32, 16, 128)
 
 
-def grid_stage(x, fold, tt, t, var):
+def grid_stage(x, fold, tt, t, sign, var):
     first = var is None
     y = jax.ShapeDtypeStruct((32, 16, 128), BF)
     return pl.pallas_call(
         functools.partial(grid_kernel, first),
-        out_shape=(y, jax.ShapeDtypeStruct((512, 128), F32)) if first else y,
-        scratch_shapes=[pltpu.VMEM((2048, 128), BF)],
-        compiler_params=pltpu.CompilerParams(vmem_limit_bytes=12 << 20),
-    )(*((x, fold, tt, t) if first else (x, fold, tt, t, var)))
+        out_shape=(y, jax.ShapeDtypeStruct((256, 256), F32)) if first else y,
+        scratch_shapes=[pltpu.VMEM((2048, 256), BF)],
+        compiler_params=pltpu.CompilerParams(vmem_limit_bytes=12 << 20),
+    )(*((x, fold, tt, t, sign) if first else (x, fold, tt, t, sign, var)))
 
 
 def forward_kernel(pid_ref, at_ref, y_ref, leg_ref, out_ref, wide_ref):
@@ -346,19 +379,18 @@
                 shift = (32 * (jj - s)) % 128
                 v = pltpu.roll(blocks[jj], shift, 1) if shift else blocks[jj]
                 lhs = v if lhs is None else jnp.where(lane >= 32 * jj, v, lhs)
-            p = jnp.dot(lhs.astype(BF), leg_ref[t], preferred_element_type=F32)
+            p = jnp.dot(lhs.astype(BF), whole(leg_ref, t), preferred_element_type=F32)
             mask = even_mask((16, RP), pid_ref[at_ref[0] + 4 * (t // 2) + t % 2])
             done.append(jnp.where(mask, p[0:16], p[16:32]))
         for u in range(2):
-            for n, v in enumerate(pack(done[2 * u : 2 * u + 2], jnp.zeros((16, 128), F32))):
-                out_ref[2 * b + u, 16 * n : 16 * n + 16, :] = v
+            put(out_ref, 2 * b + u, pack(done[2 * u : 2 * u + 2], jnp.zeros((8, 128), F32)))
 
 
 def legendre_forward(pids, at, y, leg):
     return pl.pallas_call(
         forward_kernel,
         in_specs=[SMEM, SMEM, VMEM, VMEM],
-        out_shape=jax.ShapeDtypeStruct((8, 272, 128), BF),
+        out_shape=jax.ShapeDtypeStruct((8, 264, 128), BF),
         scratch_shapes=[pltpu.VMEM((32, 16, 128), F32)],
         compiler_params=pltpu.CompilerParams(vmem_limit_bytes=12 << 20),
     )(pids, at, y, leg)
@@ -394,17 +426,15 @@
 def owner_kernel(parts_ref, table_ref, out_ref):
     sh = summed_blocks(parts_ref, table_ref)
     tile = split_tile(pltpu.roll(gram_tile(sh), 8, 1))
-    tile = jnp.concatenate([tile, jnp.zeros((8, 128), F32)], axis=0)
     pieces = pack([sh[b] * table_ref[2 + b : 3 + b, :] for b in range(2)], tile)
     for z in range(out_ref.shape[0]):
-        for n, v in enumerate(pieces):
-            out_ref[z, 16 * n : 16 * n + 16, :] = v
+        put(out_ref, z, pieces)
 
 
 def owner_step(parts, table):
     return pl.pallas_call(
         owner_kernel,
-        out_shape=jax.ShapeDtypeStruct((8, 272, 128), BF),
+        out_shape=jax.ShapeDtypeStruct((8, 264, 128), BF),
         compiler_params=pltpu.CompilerParams(vmem_limit_bytes=12 << 20),
     )(parts, table)
 
@@ -474,8 +504,8 @@
     both = combine(at, legendre, got)
     pids = pair_of_slot.reshape(16, 8, 2, 2).transpose(0, 2, 1, 3).reshape(1, 512)
     place = jnp.where(pids % 2 == 0, pids, T_SIZE - pids) // 2
-    t, tt = slot_tables(place)
-    spec, both, t, tt = lax.optimization_barrier((spec, both, t, tt))
+    t, tt, sign = slot_tables(place)
+    spec, both, t, tt, sign = lax.optimization_barrier((spec, both, t, tt, sign))
     fold = jnp.asarray(fold_matrix(), BF)
 
     for step in range(STEPS):
@@ -486,9 +516,9 @@
             x = legendre_inverse(pair_of_slot, at, spec, both)
         x = lax.all_to_all(x, ("lat", "c"), 0, 0, tiled=True)
         if step == 0:
-            y, var = grid_stage(x, fold, tt, t, None)
+            y, var = grid_stage(x, fold, tt, t, sign, None)
         else:
-            y = grid_stage(x, fold, tt, t, var)
+            y = grid_stage(x, fold, tt, t, sign, var)
         y = lax.all_to_all(y, ("lat", "c"), 0, 0, tiled=True)
         parts = legendre_forward(pair_of_slot, at, y, both)
         parts = lax.all_to_all(parts, "z", 0, 0, tiled=True)

time: 260 us -> 251 us (0.965)
  Pallas kernels: 32.6 us -> 26.3 us
  waiting for transfers between devices: 1.93 us -> 7.33 us
  blocking collectives: 198 us -> 193 us
    all_to_all x1, waiting for transfers between devices: 1.03 us -> 6.42 us  [body(): spec = lax.all_to_all(spec, 'z', 0, 0, tiled=True)]
    all_to_all x3, blocking collectives: 45.9 us -> 40.6 us  [body(): x = lax.all_to_all(x, ('lat', 'c'), 0, 0, tiled=True)]
    pallas_call x4, Pallas kernels: 8.53 us -> 4.89 us  [the longest x1 2.38 us: combine(): pl.pallas_call(combine_kernel, in_specs=[SMEM, HBM, HBM], out_specs=HBM,...]
    pallas_call x3, Pallas kernels: 9.33 us -> 6.5 us  [grid_stage(): pl.pallas_call(functools.partial(grid_kernel, first), out_shape=(y, jax.S...]
    all_to_all x2, blocking collectives: 37.5 us -> 40.2 us  [body(): spec = lax.all_to_all(spec, 'z', 0, 0, tiled=True)]
    unnamed x28 -> x24, local copies, waits for them, and re-layouts: 12.9 us -> 10.8 us
  transfers between devices with their start and end apart: 3 -> 3, of which waited for: 2 -> 2; matrix products, arithmetic and copies ran while one was open for 0% -> 0% of each run, Pallas kernels for 4% -> 2%
where the time goes in v3:
time: 251 us; the launch traced here: 250 us
  blocking collectives  193 us (77%)
  Pallas kernels  26.3 us (10%)
  local copies, waits for them, and re-layouts  11.9 us (5%)
  starting transfers between devices  11.5 us (5%)
  waiting for transfers between devices  7.33 us (3%)
    all_to_all x3, blocking collectives, body(): parts = lax.all_to_all(parts, 'z', 0, 0, tiled=True)  62 us
    all_to_all x3, blocking collectives, body(): x = lax.all_to_all(x, ('lat', 'c'), 0, 0, tiled=True)  40.6 us
    all_to_all x2, blocking collectives, body(): spec = lax.all_to_all(spec, 'z', 0, 0, tiled=True)  40.2 us
    all_to_all x3, blocking collectives, body(): y = lax.all_to_all(y, ('lat', 'c'), 0, 0, tiled=True)  33.7 us
    all_to_all x1, blocking collectives, body(): lax.all_to_all(gram.reshape(128, 1, 128), ('lat', 'z'), 0, 0, tiled=True)  16.1 us
    unnamed x24, local copies, waits for them, and re-layouts  10.8 us
    pallas_call x3, Pallas kernels, legendre_inverse(): pl.pallas_call(functools.partial(inverse_kernel, first), in_specs=[SMEM,...  6.7 us
    pallas_call x3, Pallas kernels, grid_stage(): pl.pallas_call(functools.partial(grid_kernel, first), out_shape=(y, jax.S...  6.5 us
  transfers between devices with their start and end apart: 3, of which 2 were waited for; matrix products, arithmetic and copies ran while one was open for 0% of the time, Pallas kernels for 2%

profile of v3, /device:TPU:1, one launch (start us, length us, event | category | flops | bytes accessed | tf_op | source)
XLA Modules:
  0.0 250.4 jit_solution(3682537663042943153)
XLA Ops:
  0.6 3.3 %collective-permute-start = (bf16[32,64,1025]{2,1,0:T(8,128)(2,1)}, bf16[32,64,1025]{2,1,0:T(8,128)(2,1)}, u32[]{:S(2)}, u32[]{:S(2)}) collective-permute-start(bf16[32,64,1025]{2,1,0:T(8,128)(2,1)} %leg_ref.1), channel_id=1, source_target_pairs={{0,1},{1,0},{2,3},{3,2},{4,5},{5,4},{6,7},{7,6},{8,9},{9,8},{10,11... | collective-permute-start | bytes 12595208 | tf_op jit(solution)/shard_map/ppermute | solution.py:500
  4.0 0.1 pad_add_fusion.at_ref
  4.0 0.0 copy-start.7
  4.0 0.9 copy-done.7
  4.9 0.0 copy-start.8
  4.9 0.7 copy-done.8
  5.6 1.7 shard_map.95
  7.3 6.5 %all-to-all-start = ((bf16[8,264,128]{2,1,0:T(8,128)(2,1)}), bf16[8,264,128]{2,1,0:T(8,128)(2,1)S(1)}, u32[]{:S(2)}, u32[]{:S(2)}) async-start(bf16[8,264,128]{2,1,0:T(8,128)(2,1)} %get-tuple-element.18), calls=%async_computation | async-start | bytes 1081344 | tf_op jit(solution)/shard_map/all_to_all | solution.py:502
  13.8 0.9 reshape.169
  14.7 0.1 reshape.170
  14.9 0.0 copy-start.5
  14.9 1.2 copy-done.5
  16.1 0.0 copy-start.6
  16.1 1.2 copy-done.6
  17.3 1.5 shard_map.97
  18.9 0.0 collective-permute-done.got_ref
  18.9 0.0 copy-start.3
  18.9 2.3 copy-done.3
  21.2 0.0 copy-start.9
  21.2 0.0 copy-start.10
  21.2 0.0 copy-start.11
  21.2 0.0 copy-start.4
  21.2 2.4 shard_map.96.leg_ref
  23.6 0.0 copy-start
  23.6 2.1 copy-done
  25.7 6.4 %all-to-all-done.spec_ref = bf16[8,264,128]{2,1,0:T(8,128)(2,1)S(1)} async-done(((bf16[8,264,128]{2,1,0:T(8,128)(2,1)}), bf16[8,264,128]{2,1,0:T(8,128)(2,1)S(1)}, u32[]{:S(2)}, u32[]{:S(2)}) %all-to-all-start) | async-done | bytes 540704 | tf_op jit(solution)/shard_map/all_to_all | solution.py:502
  32.1 0.0 copy-done.9
  32.1 0.0 copy-done.10
  32.1 0.0 copy-done.11
  32.2 0.0 copy-start.1
  32.2 2.3 copy-done.1
  34.5 0.0 copy-start.2
  34.5 2.2 shard_map.98
  36.7 15.7 %all_to_all.65.x_ref = bf16[32,24,128]{2,1,0:T(8,128)(2,1)S(1)} all-to-all(bf16[32,24,128]{2,1,0:T(8,128)(2,1)S(1)} %shard_map.98), channel_id=1, replica_groups=mesh['lat'=16,'z'=8,'c'=2] {'lat','c'}, dimensions={0} | all-to-all | bytes 393216 | tf_op jit(solution)/shard_map/all_to_all | solution.py:517
  52.4 0.0 copy-done.4
  52.4 2.0 shard_map.99
  54.4 11.2 %all_to_all.66.y_ref = bf16[32,16,128]{2,1,0:T(8,128)(2,1)S(1)} all-to-all(bf16[32,16,128]{2,1,0:T(8,128)(2,1)S(1)} %get-tuple-element.27), channel_id=1, replica_groups=mesh['lat'=16,'z'=8,'c'=2] {'lat','c'}, dimensions={0} | all-to-all | bytes 262144 | tf_op jit(solution)/shard_map/all_to_all | solution.py:522
  65.7 0.0 copy-done.2
  65.7 1.7 shard_map.100
  67.4 20.7 %all_to_all.67.parts_ref = bf16[8,264,128]{2,1,0:T(8,128)(2,1)S(1)} all-to-all(bf16[8,264,128]{2,1,0:T(8,128)(2,1)S(1)} %shard_map.100), channel_id=1, replica_groups=mesh['lat'=16,'z'=8,'c'=2] {'z'}, dimensions={0} | all-to-all | bytes 1081344 | tf_op jit(solution)/shard_map/all_to_all | solution.py:524
  88.0 0.5 shard_map.101
  88.5 20.1 %all_to_all.68.spec_ref = bf16[8,264,128]{2,1,0:T(8,128)(2,1)S(1)} all-to-all(bf16[8,264,128]{2,1,0:T(8,128)(2,1)S(1)} %shard_map.101), channel_id=1, replica_groups=mesh['lat'=16,'z'=8,'c'=2] {'z'}, dimensions={0} | all-to-all | bytes 1081344 | tf_op jit(solution)/shard_map/all_to_all | solution.py:515
  108.6 2.2 shard_map.102
  110.9 12.5 %all_to_all.69.x_ref = bf16[32,24,128]{2,1,0:T(8,128)(2,1)S(1)} all-to-all(bf16[32,24,128]{2,1,0:T(8,128)(2,1)S(1)} %shard_map.102), channel_id=1, replica_groups=mesh['lat'=16,'z'=8,'c'=2] {'lat','c'}, dimensions={0} | all-to-all | bytes 393216 | tf_op jit(solution)/shard_map/all_to_all | solution.py:517
  123.3 2.2 shard_map.103
  125.6 11.2 %all_to_all.70.y_ref = bf16[32,16,128]{2,1,0:T(8,128)(2,1)S(1)} all-to-all(bf16[32,16,128]{2,1,0:T(8,128)(2,1)S(1)} %shard_map.103), channel_id=1, replica_groups=mesh['lat'=16,'z'=8,'c'=2] {'lat','c'}, dimensions={0} | all-to-all | bytes 262144 | tf_op jit(solution)/shard_map/all_to_all | solution.py:522
  136.8 1.7 shard_map.104
  138.5 20.7 %all_to_all.71.parts_ref = bf16[8,264,128]{2,1,0:T(8,128)(2,1)S(1)} all-to-all(bf16[8,264,128]{2,1,0:T(8,128)(2,1)S(1)} %shard_map.104), channel_id=1, replica_groups=mesh['lat'=16,'z'=8,'c'=2] {'z'}, dimensions={0} | all-to-all | bytes 1081344 | tf_op jit(solution)/shard_map/all_to_all | solution.py:524
  159.1 0.5 shard_map.105
  159.6 20.1 %all_to_all.72.spec_ref = bf16[8,264,128]{2,1,0:T(8,128)(2,1)S(1)} all-to-all(bf16[8,264,128]{2,1,0:T(8,128)(2,1)S(1)} %shard_map.105), channel_id=1, replica_groups=mesh['lat'=16,'z'=8,'c'=2] {'z'}, dimensions={0} | all-to-all | bytes 1081344 | tf_op jit(solution)/shard_map/all_to_all | solution.py:515
  179.7 2.2 shard_map.106
  182.0 12.5 %all_to_all.73.x_ref = bf16[32,24,128]{2,1,0:T(8,128)(2,1)S(1)} all-to-all(bf16[32,24,128]{2,1,0:T(8,128)(2,1)S(1)} %shard_map.106), channel_id=1, replica_groups=mesh['lat'=16,'z'=8,'c'=2] {'lat','c'}, dimensions={0} | all-to-all | bytes 393216 | tf_op jit(solution)/shard_map/all_to_all | solution.py:517
  194.4 2.2 shard_map.107
  196.7 11.2 %all_to_all.74.y_ref = bf16[32,16,128]{2,1,0:T(8,128)(2,1)S(1)} all-to-all(bf16[32,16,128]{2,1,0:T(8,128)(2,1)S(1)} %shard_map.107), channel_id=1, replica_groups=mesh['lat'=16,'z'=8,'c'=2] {'lat','c'}, dimensions={0} | all-to-all | bytes 262144 | tf_op jit(solution)/shard_map/all_to_all | solution.py:522
  207.9 1.7 shard_map.108
  209.6 20.7 %all_to_all.75.parts_ref = bf16[8,264,128]{2,1,0:T(8,128)(2,1)S(1)} all-to-all(bf16[8,264,128]{2,1,0:T(8,128)(2,1)S(1)} %shard_map.108), channel_id=1, replica_groups=mesh['lat'=16,'z'=8,'c'=2] {'z'}, dimensions={0} | all-to-all | bytes 1081344 | tf_op jit(solution)/shard_map/all_to_all | solution.py:524
  230.3 0.4 shard_map.109
  230.7 16.1 %all_to_all.76 = f32[128,1,128]{2,1,0:T(1,128)S(1)} all-to-all(f32[128,1,128]{2,1,0:T(1,128)S(1)} %bitcast.14), channel_id=1, replica_groups=mesh['lat'=16,'z'=8,'c'=2] {'lat','z'}, dimensions={0} | all-to-all | bytes 131072 | tf_op jit(solution)/shard_map/all_to_all | solution.py:528
  246.8 1.7 collective-permute-start.1
  248.5 0.9 collective-permute-done.1.other_ref
  249.4 1.1 shard_map.110
  (2 shorter events, 0.0 us)
Async XLA Ops:
  0.6 18.2 %collective-permute-start = (bf16[32,64,1025]{2,1,0:T(8,128)(2,1)}, bf16[32,64,1025]{2,1,0:T(8,128)(2,1)}, u32[]{:S(2)}, u32[]{:S(2)}) collective-permute-start(bf16[32,64,1025]{2,1,0:T(8,128)(2,1)} %leg_ref.1), channel_id=1, source_target_pairs={{0,1},{1,0},{2,3},{3,2},{4,5},{5,4},{6,7},{7,6},{8,9},{9,8},{10,11... | collective-permute-start | bytes 12595208 | tf_op jit(solution)/shard_map/ppermute | solution.py:500
  4.0 0.9 copy-start.7
  4.9 0.7 copy-start.8
  7.3 24.8 %all-to-all-start = ((bf16[8,264,128]{2,1,0:T(8,128)(2,1)}), bf16[8,264,128]{2,1,0:T(8,128)(2,1)S(1)}, u32[]{:S(2)}, u32[]{:S(2)}) async-start(bf16[8,264,128]{2,1,0:T(8,128)(2,1)} %get-tuple-element.18), calls=%async_computation | async-start | bytes 1081344 | tf_op jit(solution)/shard_map/all_to_all | solution.py:502
  14.9 1.2 copy-start.5
  16.1 1.2 copy-start.6
  18.9 2.3 copy-start.3
  21.2 10.9 %copy-start.9 = (s32[512]{0:T(512)S(1)}, s32[512]{0:T(512)}, u32[]{:S(2)}) copy-start(s32[512]{0:T(512)} %pid_ref.13) | copy-start | bytes 6148
  21.2 10.9 %copy-start.10 = (f32[64,128]{1,0:T(8,128)S(1)}, f32[64,128]{1,0:T(8,128)}, u32[]{:S(2)}) copy-start(f32[64,128]{1,0:T(8,128)} %refs_0_.1) | copy-start | bytes 98308
  21.2 10.9 %copy-start.11 = (f32[64]{0:T(128)S(1)}, f32[64]{0:T(128)}, u32[]{:S(2)}) copy-start(f32[64]{0:T(128)} %param.11) | copy-start | bytes 772
  21.2 31.2 %copy-start.4 = (bf16[128,512]{1,0:T(8,128)(2,1)S(1)}, bf16[128,512]{1,0:T(8,128)(2,1)}, u32[]{:S(2)}) copy-start(bf16[128,512]{1,0:T(8,128)(2,1)} %constant.54.clone.fold_ref) | copy-start | bytes 393220
  23.6 2.1 copy-start
  32.2 2.3 copy-start.1
  34.5 31.2 %copy-start.2 = (bf16[16,128,1025]{2,1,0:T(8,128)(2,1)S(1)}, bf16[16,128,1025]{2,1,0:T(8,128)(2,1)}, u32[]{:S(2)}) copy-start(bf16[16,128,1025]{2,1,0:T(8,128)(2,1)} %copy-done) | copy-start | bytes 12595204
  246.8 2.6 %collective-permute-start.1 = (f32[128,128]{1,0:T(8,128)S(1)}, f32[128,128]{1,0:T(8,128)S(1)}, u32[]{:S(2)}, u32[]{:S(2)}) collective-permute-start(f32[128,128]{1,0:T(8,128)S(1)} %bitcast.12), channel_id=1, source_target_pairs={{0,1},{1,0},{2,3},{3,2},{4,5},{5,4},{6,7},{7,6},{8,9},{9,8},{10,11... | collective-permute-start | bytes 196616 | tf_op jit(solution)/shard_map/ppermute | solution.py:529

commit v4 on v3

--- a/solution.py
+++ b/solution.py
@@ -17,6 +17,8 @@
 NPAIR = 512
 R = 1025
 RP = 1152
+ORDER = [3 * i % 8 for i in range(8)]
+PLACE = [ORDER.index(i) for i in range(8)]
 BF = jnp.bfloat16
 F32 = jnp.float32
 GSCALE = 1.0 / (2.0 * NPAIR * R)
@@ -129,10 +131,9 @@
         out_ref[z, 16 * n : 16 * n + v.shape[0], :] = v
 
 
-def start_kernel(pid_ref, at_ref, start_ref, out_ref, table_ref):
-    base = at_ref[0] + at_ref[1]
+def start_kernel(at_ref, start_ref, out_ref, table_ref):
     place, row = lanes((2, RP)), rows((2, RP))
-    pid = jnp.where(row == 0, pid_ref[base], pid_ref[base + 1])
+    pid = jnp.where(row == 0, at_ref[2], at_ref[3])
     first = place < T_SIZE + 1 - pid
     degree = jnp.where(first, pid + place, place - 1)
     wave = jnp.where(first, pid, T_SIZE - pid)
@@ -166,13 +167,13 @@
 HBM = pl.BlockSpec(memory_space=pltpu.HBM)
 
 
-def start_step(pids, at, start):
+def start_step(at, start):
     return pl.pallas_call(
         start_kernel,
-        in_specs=[SMEM, SMEM, VMEM],
+        in_specs=[SMEM, VMEM],
         out_shape=(jax.ShapeDtypeStruct((8, 264, 128), BF), jax.ShapeDtypeStruct((8, RP), F32)),
         compiler_params=pltpu.CompilerParams(vmem_limit_bytes=12 << 20),
-    )(pids, at, start)
+    )(at, start)
 
 
 def table_kernel(place_ref, nat_ref, natt_ref, t_ref, tt_ref, sign_ref):
@@ -200,19 +201,33 @@
     )(place, jnp.asarray(nat.reshape(2048, 256)), jnp.asarray(natt))
 
 
-def slot_waves(spec_ref, z, b, pid, leg):
+def slot_waves(spec_ref, z, b, pid, leg_ref, t):
     lane = lanes((32, 128))
-    sp = load_block(spec_ref, z, b)
-    mask = even_mask((16, RP), pid)
+
+    def own(pieces):
+        return jnp.where(lane < 32, pieces[0], jnp.where(lane < 64, pieces[1], jnp.where(lane < 96, pieces[2], pieces[3])))
+
+    main = [spec_ref[z, (b * 8 + l) * 16 : (b * 8 + l) * 16 + 16, :].astype(F32) for l in range(8)]
+    sp = jnp.concatenate(main, axis=1)
+    mask = even_mask((16, 1024), pid)
     even = jnp.where(mask, sp, 0.0).astype(BF)
     odd = jnp.where(mask, 0.0, sp).astype(BF)
     wide = jnp.concatenate([even, odd] * 4, axis=0)
-    p = lax.dot_general(leg, wide, (((1,), (1,)), ((), ())), preferred_element_type=F32)
-    return jnp.where(lane < 32, p[0:32], jnp.where(lane < 64, p[32:64], jnp.where(lane < 96, p[64:96], p[96:128])))
+    p = lax.dot_general(leg_ref[t, :, 0:1024], wide, (((1,), (1,)), ((), ())), preferred_element_type=F32)
+    extra = spec_ref[z, 256:264, :].astype(F32)
+    lane8, row8 = lanes((8, 128)), rows((8, 128))
+    here = (lax.rem(lane8, 8) == row8) & (lax.rem(lane8 // 16, 2) == 1 - lax.rem(pid, 2))
+    line = jnp.zeros((8, 128), F32)
+    for c in range(2):
+        col = jnp.broadcast_to(extra[:, 2 * b + c : 2 * b + c + 1], (8, 128))
+        line = jnp.where(here & (lax.rem(lane8 // 8, 2) == c), col, line)
+    line = jnp.sum(line, axis=0, keepdims=True)
+    last = own([jnp.broadcast_to(leg_ref[t, 32 * jj : 32 * jj + 32, 1024:R].astype(F32), (32, 128)) for jj in range(4)])
+    return own([p[32 * jj : 32 * jj + 32] for jj in range(4)]) + last * line
 
 
 def combine_kernel(at_ref, leg_ref, got_ref, both_ref, sems):
-    core = at_ref[2]
+    core = at_ref[1]
     copies = []
     for z in range(8):
         for n, (ref, half) in enumerate(((leg_ref, core), (got_ref, 1 - core))):
@@ -265,7 +280,7 @@
         out_ref[:, 16:24, :] = jnp.broadcast_to(tile[None], (32, 8, 128))
     for t in range(16):
         pid = pid_ref[at_ref[0] + 4 * (t // 2) + t % 2]
-        acc_ref[:, t, :] = slot_waves(spec_ref, t // 2, t % 2, pid, whole(leg_ref, t))
+        acc_ref[:, t, :] = slot_waves(spec_ref, PLACE[t // 2], t % 2, pid, leg_ref, t)
     if first:
         out_ref[...] = acc_ref[...].astype(BF)
     else:
@@ -383,7 +398,7 @@
             mask = even_mask((16, RP), pid_ref[at_ref[0] + 4 * (t // 2) + t % 2])
             done.append(jnp.where(mask, p[0:16], p[16:32]))
         for u in range(2):
-            put(out_ref, 2 * b + u, pack(done[2 * u : 2 * u + 2], jnp.zeros((8, 128), F32)))
+            put(out_ref, PLACE[2 * b + u], pack(done[2 * u : 2 * u + 2], jnp.zeros((8, 128), F32)))
 
 
 def legendre_forward(pids, at, y, leg):
@@ -496,10 +511,12 @@
 
 def body(start_block, legendre, variance, gauss_weight, pair_of_slot):
     lat, zpos, core = lax.axis_index("lat"), lax.axis_index("z"), lax.axis_index("c")
-    at = jnp.stack([lat * 32 + core * 2, zpos * 4, core]).astype(jnp.int32)
+    base = lat * 32 + core * 2
+    own = lax.dynamic_slice(pair_of_slot, (base + zpos * 4,), (2,))
+    at = jnp.concatenate([jnp.stack([base, core]).astype(jnp.int32), own])
     got = lax.ppermute(legendre, "c", [(0, 1), (1, 0)])
-    spec, table = start_step(pair_of_slot, at, start_block)
-    spec = lax.all_to_all(spec, "z", 0, 0, tiled=True)
+    spec, table = start_step(at, start_block)
+    spec = lax.all_to_all(spec, "z", 0, 0, axis_index_groups=[ORDER], tiled=True)
 
     both = combine(at, legendre, got)
     pids = pair_of_slot.reshape(16, 8, 2, 2).transpose(0, 2, 1, 3).reshape(1, 512)
@@ -512,7 +529,7 @@
         if step == 0:
             x = legendre_inverse(pair_of_slot, at, spec, both, variance, gauss_weight.reshape(1, 64))
         else:
-            spec = lax.all_to_all(spec, "z", 0, 0, tiled=True)
+            spec = lax.all_to_all(spec, "z", 0, 0, axis_index_groups=[ORDER], tiled=True)
             x = legendre_inverse(pair_of_slot, at, spec, both)
         x = lax.all_to_all(x, ("lat", "c"), 0, 0, tiled=True)
         if step == 0:
@@ -521,7 +538,7 @@
             y = grid_stage(x, fold, tt, t, sign, var)
         y = lax.all_to_all(y, ("lat", "c"), 0, 0, tiled=True)
         parts = legendre_forward(pair_of_slot, at, y, both)
-        parts = lax.all_to_all(parts, "z", 0, 0, tiled=True)
+        parts = lax.all_to_all(parts, "z", 0, 0, axis_index_groups=[ORDER], tiled=True)
         if step + 1 < STEPS:
             spec = owner_step(parts, table)
     sh, gram = last_step(parts, table)

time: 251 us -> 247 us (0.984)
  waiting for transfers between devices: 7.33 us -> 4.45 us
    all_to_all x5, blocking collectives: 102 us -> 93.1 us  [the longest x3 56.6 us: body(): lax.all_to_all(parts, 'z', 0, 0, axis_index_groups=[ORDER], tiled=True)]
    all_to_all x3, blocking collectives: 40.6 us -> 47.2 us  [body(): x = lax.all_to_all(x, ('lat', 'c'), 0, 0, tiled=True)]
    all_to_all x1, waiting for transfers between devices: 6.42 us -> 3.54 us  [body(): lax.all_to_all(spec, 'z', 0, 0, axis_index_groups=[ORDER], tiled=True)]
    unnamed x24 -> x22, local copies, waits for them, and re-layouts: 10.8 us -> 10.2 us
  transfers between devices with their start and end apart: 3 -> 3, of which waited for: 2 -> 2; matrix products, arithmetic and copies ran while one was open for 0% -> 1% of each run, Pallas kernels for 2% -> 2%
where the time goes in v4:
time: 247 us; the launch traced here: 246 us
  blocking collectives  191 us (77%)
  Pallas kernels  25.3 us (10%)
  starting transfers between devices  12.3 us (5%)
  local copies, waits for them, and re-layouts  12 us (5%)
  waiting for transfers between devices  4.45 us (2%)
    all_to_all x3, blocking collectives, body(): lax.all_to_all(parts, 'z', 0, 0, axis_index_groups=[ORDER], tiled=True)  56.6 us
    all_to_all x3, blocking collectives, body(): x = lax.all_to_all(x, ('lat', 'c'), 0, 0, tiled=True)  47.2 us
    all_to_all x2, blocking collectives, body(): lax.all_to_all(spec, 'z', 0, 0, axis_index_groups=[ORDER], tiled=True)  36.5 us
    all_to_all x3, blocking collectives, body(): y = lax.all_to_all(y, ('lat', 'c'), 0, 0, tiled=True)  33.7 us
    all_to_all x1, blocking collectives, body(): lax.all_to_all(gram.reshape(128, 1, 128), ('lat', 'z'), 0, 0, tiled=True)  17 us
    unnamed x22, local copies, waits for them, and re-layouts  10.2 us
    pallas_call x3, Pallas kernels, grid_stage(): pl.pallas_call(functools.partial(grid_kernel, first), out_shape=(y, jax.S...  6.48 us
    all_to_all x1, starting transfers between devices, body(): lax.all_to_all(spec, 'z', 0, 0, axis_index_groups=[ORDER], tiled=True)  6.45 us
  transfers between devices with their start and end apart: 3, of which 2 were waited for; matrix products, arithmetic and copies ran while one was open for 1% of the time, Pallas kernels for 2%

profile of v4, /device:TPU:1, one launch (start us, length us, event | category | flops | bytes accessed | tf_op | source)
XLA Modules:
  0.0 245.9 jit_solution(13525927504456614761)
XLA Ops:
  0.6 3.3 %collective-permute-start = (bf16[32,64,1025]{2,1,0:T(8,128)(2,1)}, bf16[32,64,1025]{2,1,0:T(8,128)(2,1)}, u32[]{:S(2)}, u32[]{:S(2)}) collective-permute-start(bf16[32,64,1025]{2,1,0:T(8,128)(2,1)} %leg_ref.1), channel_id=1, source_target_pairs={{0,1},{1,0},{2,3},{3,2},{4,5},{5,4},{6,7},{7,6},{8,9},{9,8},{10,11... | collective-permute-start | bytes 12595208 | tf_op jit(solution)/shard_map/ppermute | solution.py:517
  4.0 0.8 dynamic_slice.3
  4.7 0.1 pad_add_fusion.at_ref
  4.8 0.0 copy-start.7
  4.8 0.9 copy-done.7
  5.7 1.7 shard_map.95
  7.4 6.5 %all-to-all-start = ((bf16[8,264,128]{2,1,0:T(8,128)(2,1)}), bf16[8,264,128]{2,1,0:T(8,128)(2,1)S(1)}, u32[]{:S(2)}, u32[]{:S(2)}) async-start(bf16[8,264,128]{2,1,0:T(8,128)(2,1)} %get-tuple-element.18), calls=%async_computation | async-start | bytes 1081344 | tf_op jit(solution)/shard_map/all_to_all | solution.py:519
  13.8 0.9 reshape.169
  14.7 0.1 reshape.170
  14.9 0.0 copy-start.5
  14.9 1.2 copy-done.5
  16.1 0.0 copy-start.6
  16.1 1.2 copy-done.6
  17.4 1.5 shard_map.97
  18.9 0.0 collective-permute-done.got_ref
  18.9 0.0 copy-start.3
  18.9 2.3 copy-done.3
  21.2 0.0 copy-start.8
  21.2 0.0 copy-start.9
  21.2 0.0 copy-start.10
  21.3 0.0 copy-start.4
  21.3 2.4 shard_map.96.leg_ref
  23.6 0.0 copy-start
  23.6 2.1 copy-done
  25.8 3.5 %all-to-all-done.spec_ref = bf16[8,264,128]{2,1,0:T(8,128)(2,1)S(1)} async-done(((bf16[8,264,128]{2,1,0:T(8,128)(2,1)}), bf16[8,264,128]{2,1,0:T(8,128)(2,1)S(1)}, u32[]{:S(2)}, u32[]{:S(2)}) %all-to-all-start) | async-done | bytes 540704 | tf_op jit(solution)/shard_map/all_to_all | solution.py:519
  29.3 0.0 copy-done.8
  29.3 0.0 copy-done.9
  29.3 0.0 copy-done.10
  29.3 0.0 copy-start.1
  29.3 2.3 copy-done.1
  31.7 0.0 copy-start.2
  31.7 2.0 shard_map.98
  33.6 17.1 %all_to_all.65.x_ref = bf16[32,24,128]{2,1,0:T(8,128)(2,1)S(1)} all-to-all(bf16[32,24,128]{2,1,0:T(8,128)(2,1)S(1)} %shard_map.98), channel_id=1, replica_groups=mesh['lat'=16,'z'=8,'c'=2] {'lat','c'}, dimensions={0} | all-to-all | bytes 393216 | tf_op jit(solution)/shard_map/all_to_all | solution.py:534
  50.8 0.0 copy-done.4
  50.8 2.0 shard_map.99
  52.8 11.2 %all_to_all.66.y_ref = bf16[32,16,128]{2,1,0:T(8,128)(2,1)S(1)} all-to-all(bf16[32,16,128]{2,1,0:T(8,128)(2,1)S(1)} %get-tuple-element.27), channel_id=1, replica_groups=mesh['lat'=16,'z'=8,'c'=2] {'lat','c'}, dimensions={0} | all-to-all | bytes 262144 | tf_op jit(solution)/shard_map/all_to_all | solution.py:539
  64.0 0.0 copy-done.2
  64.0 1.7 shard_map.100
  65.7 18.9 %all_to_all.67.parts_ref = bf16[8,264,128]{2,1,0:T(8,128)(2,1)S(1)} all-to-all(bf16[8,264,128]{2,1,0:T(8,128)(2,1)S(1)} %shard_map.100), channel_id=1, replica_groups={{0,6,12,2,8,14,4,10},{1,7,13,3,9,15,5,11},{16,22,28,18,24,30,20,26},{17..., dimensions={0} | all-to-all | bytes 1081344 | tf_op jit(solution)/shard_map/all_to_all | solution.py:541
  84.6 0.5 shard_map.101
  85.1 18.5 %all_to_all.68.spec_ref = bf16[8,264,128]{2,1,0:T(8,128)(2,1)S(1)} all-to-all(bf16[8,264,128]{2,1,0:T(8,128)(2,1)S(1)} %shard_map.101), channel_id=1, replica_groups={{0,6,12,2,8,14,4,10},{1,7,13,3,9,15,5,11},{16,22,28,18,24,30,20,26},{17..., dimensions={0} | all-to-all | bytes 1081344 | tf_op jit(solution)/shard_map/all_to_all | solution.py:532
  103.5 1.9 shard_map.102
  105.5 15.0 %all_to_all.69.x_ref = bf16[32,24,128]{2,1,0:T(8,128)(2,1)S(1)} all-to-all(bf16[32,24,128]{2,1,0:T(8,128)(2,1)S(1)} %shard_map.102), channel_id=1, replica_groups=mesh['lat'=16,'z'=8,'c'=2] {'lat','c'}, dimensions={0} | all-to-all | bytes 393216 | tf_op jit(solution)/shard_map/all_to_all | solution.py:534
  120.5 2.2 shard_map.103
  122.7 11.2 %all_to_all.70.y_ref = bf16[32,16,128]{2,1,0:T(8,128)(2,1)S(1)} all-to-all(bf16[32,16,128]{2,1,0:T(8,128)(2,1)S(1)} %shard_map.103), channel_id=1, replica_groups=mesh['lat'=16,'z'=8,'c'=2] {'lat','c'}, dimensions={0} | all-to-all | bytes 262144 | tf_op jit(solution)/shard_map/all_to_all | solution.py:539
  133.9 1.7 shard_map.104
  135.6 18.8 %all_to_all.71.parts_ref = bf16[8,264,128]{2,1,0:T(8,128)(2,1)S(1)} all-to-all(bf16[8,264,128]{2,1,0:T(8,128)(2,1)S(1)} %shard_map.104), channel_id=1, replica_groups={{0,6,12,2,8,14,4,10},{1,7,13,3,9,15,5,11},{16,22,28,18,24,30,20,26},{17..., dimensions={0} | all-to-all | bytes 1081344 | tf_op jit(solution)/shard_map/all_to_all | solution.py:541
  154.5 0.5 shard_map.105
  154.9 18.0 %all_to_all.72.spec_ref = bf16[8,264,128]{2,1,0:T(8,128)(2,1)S(1)} all-to-all(bf16[8,264,128]{2,1,0:T(8,128)(2,1)S(1)} %shard_map.105), channel_id=1, replica_groups={{0,6,12,2,8,14,4,10},{1,7,13,3,9,15,5,11},{16,22,28,18,24,30,20,26},{17..., dimensions={0} | all-to-all | bytes 1081344 | tf_op jit(solution)/shard_map/all_to_all | solution.py:532
  173.0 1.9 shard_map.106
  174.9 15.1 %all_to_all.73.x_ref = bf16[32,24,128]{2,1,0:T(8,128)(2,1)S(1)} all-to-all(bf16[32,24,128]{2,1,0:T(8,128)(2,1)S(1)} %shard_map.106), channel_id=1, replica_groups=mesh['lat'=16,'z'=8,'c'=2] {'lat','c'}, dimensions={0} | all-to-all | bytes 393216 | tf_op jit(solution)/shard_map/all_to_all | solution.py:534
  190.0 2.2 shard_map.107
  192.2 11.2 %all_to_all.74.y_ref = bf16[32,16,128]{2,1,0:T(8,128)(2,1)S(1)} all-to-all(bf16[32,16,128]{2,1,0:T(8,128)(2,1)S(1)} %shard_map.107), channel_id=1, replica_groups=mesh['lat'=16,'z'=8,'c'=2] {'lat','c'}, dimensions={0} | all-to-all | bytes 262144 | tf_op jit(solution)/shard_map/all_to_all | solution.py:539
  203.4 1.7 shard_map.108
  205.1 18.8 %all_to_all.75.parts_ref = bf16[8,264,128]{2,1,0:T(8,128)(2,1)S(1)} all-to-all(bf16[8,264,128]{2,1,0:T(8,128)(2,1)S(1)} %shard_map.108), channel_id=1, replica_groups={{0,6,12,2,8,14,4,10},{1,7,13,3,9,15,5,11},{16,22,28,18,24,30,20,26},{17..., dimensions={0} | all-to-all | bytes 1081344 | tf_op jit(solution)/shard_map/all_to_all | solution.py:541
  224.0 0.4 shard_map.109
  224.4 17.0 %all_to_all.76 = f32[128,1,128]{2,1,0:T(1,128)S(1)} all-to-all(f32[128,1,128]{2,1,0:T(1,128)S(1)} %bitcast.13), channel_id=1, replica_groups=mesh['lat'=16,'z'=8,'c'=2] {'lat','z'}, dimensions={0} | all-to-all | bytes 131072 | tf_op jit(solution)/shard_map/all_to_all | solution.py:545
  241.4 2.5 %collective-permute-start.1 = (f32[128,128]{1,0:T(8,128)S(1)}, f32[128,128]{1,0:T(8,128)S(1)}, u32[]{:S(2)}, u32[]{:S(2)}) collective-permute-start(f32[128,128]{1,0:T(8,128)S(1)} %bitcast.11), channel_id=1, source_target_pairs={{0,1},{1,0},{2,3},{3,2},{4,5},{5,4},{6,7},{7,6},{8,9},{9,8},{10,11... | collective-permute-start | bytes 196616 | tf_op jit(solution)/shard_map/ppermute | solution.py:546
  243.9 0.9 collective-permute-done.1.other_ref
  244.8 1.1 shard_map.110
  (2 shorter events, 0.0 us)
Async XLA Ops:
  0.6 18.3 %collective-permute-start = (bf16[32,64,1025]{2,1,0:T(8,128)(2,1)}, bf16[32,64,1025]{2,1,0:T(8,128)(2,1)}, u32[]{:S(2)}, u32[]{:S(2)}) collective-permute-start(bf16[32,64,1025]{2,1,0:T(8,128)(2,1)} %leg_ref.1), channel_id=1, source_target_pairs={{0,1},{1,0},{2,3},{3,2},{4,5},{5,4},{6,7},{7,6},{8,9},{9,8},{10,11... | collective-permute-start | bytes 12595208 | tf_op jit(solution)/shard_map/ppermute | solution.py:517
  4.8 0.9 copy-start.7
  7.4 22.0 %all-to-all-start = ((bf16[8,264,128]{2,1,0:T(8,128)(2,1)}), bf16[8,264,128]{2,1,0:T(8,128)(2,1)S(1)}, u32[]{:S(2)}, u32[]{:S(2)}) async-start(bf16[8,264,128]{2,1,0:T(8,128)(2,1)} %get-tuple-element.18), calls=%async_computation | async-start | bytes 1081344 | tf_op jit(solution)/shard_map/all_to_all | solution.py:519
  14.9 1.2 copy-start.5
  16.1 1.2 copy-start.6
  18.9 2.3 copy-start.3
  21.2 8.1 %copy-start.8 = (s32[512]{0:T(512)S(1)}, s32[512]{0:T(512)}, u32[]{:S(2)}) copy-start(s32[512]{0:T(512)} %pid_ref.11) | copy-start | bytes 6148
  21.2 8.1 %copy-start.9 = (f32[64,128]{1,0:T(8,128)S(1)}, f32[64,128]{1,0:T(8,128)}, u32[]{:S(2)}) copy-start(f32[64,128]{1,0:T(8,128)} %refs_0_.1) | copy-start | bytes 98308
  21.2 8.1 %copy-start.10 = (f32[64]{0:T(128)S(1)}, f32[64]{0:T(128)}, u32[]{:S(2)}) copy-start(f32[64]{0:T(128)} %param.11) | copy-start | bytes 772
  21.3 29.5 %copy-start.4 = (bf16[128,512]{1,0:T(8,128)(2,1)S(1)}, bf16[128,512]{1,0:T(8,128)(2,1)}, u32[]{:S(2)}) copy-start(bf16[128,512]{1,0:T(8,128)(2,1)} %constant.57.clone.fold_ref) | copy-start | bytes 393220
  23.6 2.1 copy-start
  29.3 2.3 copy-start.1
  31.7 32.4 %copy-start.2 = (bf16[16,128,1025]{2,1,0:T(8,128)(2,1)S(1)}, bf16[16,128,1025]{2,1,0:T(8,128)(2,1)}, u32[]{:S(2)}) copy-start(bf16[16,128,1025]{2,1,0:T(8,128)(2,1)} %copy-done) | copy-start | bytes 12595204
  241.4 3.4 %collective-permute-start.1 = (f32[128,128]{1,0:T(8,128)S(1)}, f32[128,128]{1,0:T(8,128)S(1)}, u32[]{:S(2)}, u32[]{:S(2)}) collective-permute-start(f32[128,128]{1,0:T(8,128)S(1)} %bitcast.11), channel_id=1, source_target_pairs={{0,1},{1,0},{2,3},{3,2},{4,5},{5,4},{6,7},{7,6},{8,9},{9,8},{10,11... | collective-permute-start | bytes 196616 | tf_op jit(solution)/shard_map/ppermute | solution.py:546

commit v5 on v4

--- a/solution.py
+++ b/solution.py
@@ -17,7 +17,7 @@
 NPAIR = 512
 R = 1025
 RP = 1152
-ORDER = [3 * i % 8 for i in range(8)]
+ORDER = [0, 1, 4, 5, 2, 3, 6, 7]
 PLACE = [ORDER.index(i) for i in range(8)]
 BF = jnp.bfloat16
 F32 = jnp.float32
@@ -212,7 +212,7 @@
     mask = even_mask((16, 1024), pid)
     even = jnp.where(mask, sp, 0.0).astype(BF)
     odd = jnp.where(mask, 0.0, sp).astype(BF)
-    wide = jnp.concatenate([even, odd] * 4, axis=0)
+    wide = jnp.concatenate([even, odd], axis=0)
     p = lax.dot_general(leg_ref[t, :, 0:1024], wide, (((1,), (1,)), ((), ())), preferred_element_type=F32)
     extra = spec_ref[z, 256:264, :].astype(F32)
     lane8, row8 = lanes((8, 128)), rows((8, 128))
@@ -223,7 +223,7 @@
         line = jnp.where(here & (lax.rem(lane8 // 8, 2) == c), col, line)
     line = jnp.sum(line, axis=0, keepdims=True)
     last = own([jnp.broadcast_to(leg_ref[t, 32 * jj : 32 * jj + 32, 1024:R].astype(F32), (32, 128)) for jj in range(4)])
-    return own([p[32 * jj : 32 * jj + 32] for jj in range(4)]) + last * line
+    return jnp.concatenate([p[32 * jj : 32 * jj + 32] for jj in range(4)], axis=1) + last * line
 
 
 def combine_kernel(at_ref, leg_ref, got_ref, both_ref, sems):

time: 247 us -> 246 us (level)
    all_to_all x2, blocking collectives: 36.5 us -> 32.7 us  [body(): lax.all_to_all(spec, 'z', 0, 0, axis_index_groups=[ORDER], tiled=True)]
where the time goes in v5:
time: 246 us; the launch traced here: 245 us
  blocking collectives  191 us (78%)
  Pallas kernels  25.4 us (10%)
  starting transfers between devices  12.4 us (5%)
  local copies, waits for them, and re-layouts  12 us (5%)
  waiting for transfers between devices  3.6 us (1%)
    all_to_all x3, blocking collectives, body(): lax.all_to_all(parts, 'z', 0, 0, axis_index_groups=[ORDER], tiled=True)  59 us
    all_to_all x3, blocking collectives, body(): x = lax.all_to_all(x, ('lat', 'c'), 0, 0, tiled=True)  49.3 us
    all_to_all x3, blocking collectives, body(): y = lax.all_to_all(y, ('lat', 'c'), 0, 0, tiled=True)  33.7 us
    all_to_all x2, blocking collectives, body(): lax.all_to_all(spec, 'z', 0, 0, axis_index_groups=[ORDER], tiled=True)  32.7 us
    all_to_all x1, blocking collectives, body(): lax.all_to_all(gram.reshape(128, 1, 128), ('lat', 'z'), 0, 0, tiled=True)  16.5 us
    unnamed x22, local copies, waits for them, and re-layouts  10.2 us
    pallas_call x3, Pallas kernels, grid_stage(): pl.pallas_call(functools.partial(grid_kernel, first), out_shape=(y, jax.S...  6.48 us
    all_to_all x1, starting transfers between devices, body(): lax.all_to_all(spec, 'z', 0, 0, axis_index_groups=[ORDER], tiled=True)  6.45 us
  transfers between devices with their start and end apart: 3, of which 2 were waited for; matrix products, arithmetic and copies ran while one was open for 1% of the time, Pallas kernels for 2%

profile of v5, /device:TPU:1, one launch (start us, length us, event | category | flops | bytes accessed | tf_op | source)
XLA Modules:
  0.0 245.5 jit_solution(16965209076545395953)
XLA Ops:
  0.6 3.3 %collective-permute-start = (bf16[32,64,1025]{2,1,0:T(8,128)(2,1)}, bf16[32,64,1025]{2,1,0:T(8,128)(2,1)}, u32[]{:S(2)}, u32[]{:S(2)}) collective-permute-start(bf16[32,64,1025]{2,1,0:T(8,128)(2,1)} %leg_ref.1), channel_id=1, source_target_pairs={{0,1},{1,0},{2,3},{3,2},{4,5},{5,4},{6,7},{7,6},{8,9},{9,8},{10,11... | collective-permute-start | bytes 12595208 | tf_op jit(solution)/shard_map/ppermute | solution.py:517
  4.0 0.8 dynamic_slice.3
  4.7 0.1 pad_add_fusion.at_ref
  4.8 0.0 copy-start.7
  4.8 0.9 copy-done.7
  5.7 1.7 shard_map.95
  7.4 6.5 %all-to-all-start = ((bf16[8,264,128]{2,1,0:T(8,128)(2,1)}), bf16[8,264,128]{2,1,0:T(8,128)(2,1)S(1)}, u32[]{:S(2)}, u32[]{:S(2)}) async-start(bf16[8,264,128]{2,1,0:T(8,128)(2,1)} %get-tuple-element.18), calls=%async_computation | async-start | bytes 1081344 | tf_op jit(solution)/shard_map/all_to_all | solution.py:519
  13.8 0.9 reshape.169
  14.7 0.1 reshape.170
  14.9 0.0 copy-start.5
  14.9 1.2 copy-done.5
  16.1 0.0 copy-start.6
  16.1 1.2 copy-done.6
  17.4 1.5 shard_map.97
  18.9 0.0 collective-permute-done.got_ref
  18.9 0.0 copy-start.3
  18.9 2.3 copy-done.3
  21.2 0.0 copy-start.8
  21.2 0.0 copy-start.9
  21.2 0.0 copy-start.10
  21.3 0.0 copy-start.4
  21.3 2.4 shard_map.96.leg_ref
  23.6 0.0 copy-start
  23.6 2.1 copy-done
  25.8 2.7 %all-to-all-done.spec_ref = bf16[8,264,128]{2,1,0:T(8,128)(2,1)S(1)} async-done(((bf16[8,264,128]{2,1,0:T(8,128)(2,1)}), bf16[8,264,128]{2,1,0:T(8,128)(2,1)S(1)}, u32[]{:S(2)}, u32[]{:S(2)}) %all-to-all-start) | async-done | bytes 540704 | tf_op jit(solution)/shard_map/all_to_all | solution.py:519
  28.5 0.0 copy-done.8
  28.5 0.0 copy-done.9
  28.5 0.0 copy-done.10
  28.5 0.0 copy-start.1
  28.5 2.3 copy-done.1
  30.8 0.0 copy-start.2
  30.8 2.0 shard_map.98
  32.8 16.9 %all_to_all.65.x_ref = bf16[32,24,128]{2,1,0:T(8,128)(2,1)S(1)} all-to-all(bf16[32,24,128]{2,1,0:T(8,128)(2,1)S(1)} %shard_map.98), channel_id=1, replica_groups=mesh['lat'=16,'z'=8,'c'=2] {'lat','c'}, dimensions={0} | all-to-all | bytes 393216 | tf_op jit(solution)/shard_map/all_to_all | solution.py:534
  49.7 0.0 copy-done.4
  49.7 2.0 shard_map.99
  51.7 11.2 %all_to_all.66.y_ref = bf16[32,16,128]{2,1,0:T(8,128)(2,1)S(1)} all-to-all(bf16[32,16,128]{2,1,0:T(8,128)(2,1)S(1)} %get-tuple-element.27), channel_id=1, replica_groups=mesh['lat'=16,'z'=8,'c'=2] {'lat','c'}, dimensions={0} | all-to-all | bytes 262144 | tf_op jit(solution)/shard_map/all_to_all | solution.py:539
  63.0 0.0 copy-done.2
  63.0 1.7 shard_map.100
  64.6 20.5 %all_to_all.67.parts_ref = bf16[8,264,128]{2,1,0:T(8,128)(2,1)S(1)} all-to-all(bf16[8,264,128]{2,1,0:T(8,128)(2,1)S(1)} %shard_map.100), channel_id=1, replica_groups={{0,2,8,10,4,6,12,14},{1,3,9,11,5,7,13,15},{16,18,24,26,20,22,28,30},{17..., dimensions={0} | all-to-all | bytes 1081344 | tf_op jit(solution)/shard_map/all_to_all | solution.py:541
  85.2 0.5 shard_map.101
  85.7 16.1 %all_to_all.68.spec_ref = bf16[8,264,128]{2,1,0:T(8,128)(2,1)S(1)} all-to-all(bf16[8,264,128]{2,1,0:T(8,128)(2,1)S(1)} %shard_map.101), channel_id=1, replica_groups={{0,2,8,10,4,6,12,14},{1,3,9,11,5,7,13,15},{16,18,24,26,20,22,28,30},{17..., dimensions={0} | all-to-all | bytes 1081344 | tf_op jit(solution)/shard_map/all_to_all | solution.py:532
  101.8 1.9 shard_map.102
  103.7 16.4 %all_to_all.69.x_ref = bf16[32,24,128]{2,1,0:T(8,128)(2,1)S(1)} all-to-all(bf16[32,24,128]{2,1,0:T(8,128)(2,1)S(1)} %shard_map.102), channel_id=1, replica_groups=mesh['lat'=16,'z'=8,'c'=2] {'lat','c'}, dimensions={0} | all-to-all | bytes 393216 | tf_op jit(solution)/shard_map/all_to_all | solution.py:534
  120.1 2.2 shard_map.103
  122.4 11.2 %all_to_all.70.y_ref = bf16[32,16,128]{2,1,0:T(8,128)(2,1)S(1)} all-to-all(bf16[32,16,128]{2,1,0:T(8,128)(2,1)S(1)} %shard_map.103), channel_id=1, replica_groups=mesh['lat'=16,'z'=8,'c'=2] {'lat','c'}, dimensions={0} | all-to-all | bytes 262144 | tf_op jit(solution)/shard_map/all_to_all | solution.py:539
  133.6 1.7 shard_map.104
  135.3 19.2 %all_to_all.71.parts_ref = bf16[8,264,128]{2,1,0:T(8,128)(2,1)S(1)} all-to-all(bf16[8,264,128]{2,1,0:T(8,128)(2,1)S(1)} %shard_map.104), channel_id=1, replica_groups={{0,2,8,10,4,6,12,14},{1,3,9,11,5,7,13,15},{16,18,24,26,20,22,28,30},{17..., dimensions={0} | all-to-all | bytes 1081344 | tf_op jit(solution)/shard_map/all_to_all | solution.py:541
  154.5 0.5 shard_map.105
  155.0 16.6 %all_to_all.72.spec_ref = bf16[8,264,128]{2,1,0:T(8,128)(2,1)S(1)} all-to-all(bf16[8,264,128]{2,1,0:T(8,128)(2,1)S(1)} %shard_map.105), channel_id=1, replica_groups={{0,2,8,10,4,6,12,14},{1,3,9,11,5,7,13,15},{16,18,24,26,20,22,28,30},{17..., dimensions={0} | all-to-all | bytes 1081344 | tf_op jit(solution)/shard_map/all_to_all | solution.py:532
  171.6 2.0 shard_map.106
  173.6 15.9 %all_to_all.73.x_ref = bf16[32,24,128]{2,1,0:T(8,128)(2,1)S(1)} all-to-all(bf16[32,24,128]{2,1,0:T(8,128)(2,1)S(1)} %shard_map.106), channel_id=1, replica_groups=mesh['lat'=16,'z'=8,'c'=2] {'lat','c'}, dimensions={0} | all-to-all | bytes 393216 | tf_op jit(solution)/shard_map/all_to_all | solution.py:534
  189.5 2.2 shard_map.107
  191.8 11.2 %all_to_all.74.y_ref = bf16[32,16,128]{2,1,0:T(8,128)(2,1)S(1)} all-to-all(bf16[32,16,128]{2,1,0:T(8,128)(2,1)S(1)} %shard_map.107), channel_id=1, replica_groups=mesh['lat'=16,'z'=8,'c'=2] {'lat','c'}, dimensions={0} | all-to-all | bytes 262144 | tf_op jit(solution)/shard_map/all_to_all | solution.py:539
  203.0 1.7 shard_map.108
  204.7 19.2 %all_to_all.75.parts_ref = bf16[8,264,128]{2,1,0:T(8,128)(2,1)S(1)} all-to-all(bf16[8,264,128]{2,1,0:T(8,128)(2,1)S(1)} %shard_map.108), channel_id=1, replica_groups={{0,2,8,10,4,6,12,14},{1,3,9,11,5,7,13,15},{16,18,24,26,20,22,28,30},{17..., dimensions={0} | all-to-all | bytes 1081344 | tf_op jit(solution)/shard_map/all_to_all | solution.py:541
  223.9 0.4 shard_map.109
  224.3 16.5 %all_to_all.76 = f32[128,1,128]{2,1,0:T(1,128)S(1)} all-to-all(f32[128,1,128]{2,1,0:T(1,128)S(1)} %bitcast.13), channel_id=1, replica_groups=mesh['lat'=16,'z'=8,'c'=2] {'lat','z'}, dimensions={0} | all-to-all | bytes 131072 | tf_op jit(solution)/shard_map/all_to_all | solution.py:545
  240.8 2.6 %collective-permute-start.1 = (f32[128,128]{1,0:T(8,128)S(1)}, f32[128,128]{1,0:T(8,128)S(1)}, u32[]{:S(2)}, u32[]{:S(2)}) collective-permute-start(f32[128,128]{1,0:T(8,128)S(1)} %bitcast.11), channel_id=1, source_target_pairs={{0,1},{1,0},{2,3},{3,2},{4,5},{5,4},{6,7},{7,6},{8,9},{9,8},{10,11... | collective-permute-start | bytes 196616 | tf_op jit(solution)/shard_map/ppermute | solution.py:546
  243.5 0.9 collective-permute-done.1.other_ref
  244.4 1.1 shard_map.110
  (2 shorter events, 0.0 us)
Async XLA Ops:
  0.6 18.3 %collective-permute-start = (bf16[32,64,1025]{2,1,0:T(8,128)(2,1)}, bf16[32,64,1025]{2,1,0:T(8,128)(2,1)}, u32[]{:S(2)}, u32[]{:S(2)}) collective-permute-start(bf16[32,64,1025]{2,1,0:T(8,128)(2,1)} %leg_ref.1), channel_id=1, source_target_pairs={{0,1},{1,0},{2,3},{3,2},{4,5},{5,4},{6,7},{7,6},{8,9},{9,8},{10,11... | collective-permute-start | bytes 12595208 | tf_op jit(solution)/shard_map/ppermute | solution.py:517
  4.8 0.9 copy-start.7
  7.4 21.1 %all-to-all-start = ((bf16[8,264,128]{2,1,0:T(8,128)(2,1)}), bf16[8,264,128]{2,1,0:T(8,128)(2,1)S(1)}, u32[]{:S(2)}, u32[]{:S(2)}) async-start(bf16[8,264,128]{2,1,0:T(8,128)(2,1)} %get-tuple-element.18), calls=%async_computation | async-start | bytes 1081344 | tf_op jit(solution)/shard_map/all_to_all | solution.py:519
  14.9 1.2 copy-start.5
  16.1 1.2 copy-start.6
  18.9 2.3 copy-start.3
  21.2 7.2 %copy-start.8 = (s32[512]{0:T(512)S(1)}, s32[512]{0:T(512)}, u32[]{:S(2)}) copy-start(s32[512]{0:T(512)} %pid_ref.11) | copy-start | bytes 6148
  21.2 7.2 %copy-start.9 = (f32[64,128]{1,0:T(8,128)S(1)}, f32[64,128]{1,0:T(8,128)}, u32[]{:S(2)}) copy-start(f32[64,128]{1,0:T(8,128)} %refs_0_.1) | copy-start | bytes 98308
  21.2 7.2 %copy-start.10 = (f32[64]{0:T(128)S(1)}, f32[64]{0:T(128)}, u32[]{:S(2)}) copy-start(f32[64]{0:T(128)} %param.11) | copy-start | bytes 772
  21.3 28.4 %copy-start.4 = (bf16[128,512]{1,0:T(8,128)(2,1)S(1)}, bf16[128,512]{1,0:T(8,128)(2,1)}, u32[]{:S(2)}) copy-start(bf16[128,512]{1,0:T(8,128)(2,1)} %constant.57.clone.fold_ref) | copy-start | bytes 393220
  23.6 2.1 copy-start
  28.5 2.3 copy-start.1
  30.8 32.2 %copy-start.2 = (bf16[16,128,1025]{2,1,0:T(8,128)(2,1)S(1)}, bf16[16,128,1025]{2,1,0:T(8,128)(2,1)}, u32[]{:S(2)}) copy-start(bf16[16,128,1025]{2,1,0:T(8,128)(2,1)} %copy-done) | copy-start | bytes 12595204
  240.8 3.5 %collective-permute-start.1 = (f32[128,128]{1,0:T(8,128)S(1)}, f32[128,128]{1,0:T(8,128)S(1)}, u32[]{:S(2)}, u32[]{:S(2)}) collective-permute-start(f32[128,128]{1,0:T(8,128)S(1)} %bitcast.11), channel_id=1, source_target_pairs={{0,1},{1,0},{2,3},{3,2},{4,5},{5,4},{6,7},{7,6},{8,9},{9,8},{10,11... | collective-permute-start | bytes 196616 | tf_op jit(solution)/shard_map/ppermute | solution.py:546
